TPU v7x, 512 devices: a whole 4x8x8 slice. The times are simulated.
512 devices in a mesh: group: 4 (over z_lo), seq: 16 (over y, core), tp: 8 (over z_hi, x).
Axes of the slice: x: 4, y: 8, z: 8 (z_hi: 2, z_lo: 4; z = z_hi * 4 + z_lo), core: 2. Of those that a mesh axis runs over, the one named last changes fastest.
Arguments:
- queries: bfloat16 [8192, 8, 8, 128], P('seq', 'tp', 'group'), may hold values from -384 to 384
- aug_states: bfloat16 [8192, 5120], P('seq', ('group', 'tp')), may hold values from -6 to 6
- key_value_weight: bfloat16 [5120, 8, 2, 128], P(('group', 'tp')), may hold values from -0.078125 to 0.078125
- block_order: int32 [32], replicated, may hold values from 0 to 31, each once
Outputs:
- context: bfloat16 [8192, 8, 8, 128], P('seq', 'tp', 'group')
Inputs may be any that keep to these rules, and one draw needn't show every extreme that they name: `block_order`: each storage block number appears once.
All inputs are finite; a program needn't handle non-finite values.
Results may differ from a plain program's by a relative error of at most 0.01.
The roundings to bfloat16 on the way count: a program that leaves them out, or rounds other values in their place, can miss the bound.
Values may be sent and summed in bfloat16 or wider, within the bound.
A program may use at most 128 MiB of HBM per device.

v0:
```python
import jax
import jax.numpy as jnp
from jax import lax
from jax.sharding import PartitionSpec as P


def place_rows(row_ids, block_order, half):
    block = row_ids // half
    table = jnp.arange(block_order.shape[0], dtype=jnp.int32)
    match = block[:, None] == table[None, :]
    start_block = jnp.sum(jnp.where(match, block_order[None, :], 0), axis=1)
    return start_block * half + row_ids % half


def body(queries, aug_states, key_value_weight, block_order):
    tok = queries.shape[0]
    kv_local = queries.shape[1]
    head_size = queries.shape[3]
    feat_rows = key_value_weight.shape[0]
    part_sum = jnp.dot(
        aug_states,
        key_value_weight.reshape(feat_rows, kv_local * lax.axis_size("tp") * 2 * head_size),
        preferred_element_type=jnp.float32,
    )
    partial_kv = lax.psum_scatter(
        jnp.transpose(
            part_sum.reshape(tok, kv_local * lax.axis_size("tp"), 2, head_size), (1, 2, 0, 3)
        ),
        "tp",
        scatter_dimension=0,
        tiled=True,
    )
    key_values = lax.psum(partial_kv, "group").astype(jnp.bfloat16)
    half = tok // 2
    own_rows = lax.axis_index("seq") * tok + jnp.arange(tok, dtype=jnp.int32)
    query_pos = place_rows(own_rows, block_order, half)
    query_heads = jnp.transpose(queries, (1, 2, 0, 3))
    scale = head_size ** (-0.5)
    shape_stats = query_heads.shape[:3]
    piece = lax.all_gather(key_values, "seq", axis=2, tiled=True)
    count = piece.shape[2]
    key_pos = place_rows(jnp.arange(count, dtype=jnp.int32), block_order, half)
    top = jnp.full(shape_stats, -1e30, jnp.float32)
    scores = (
        jnp.einsum("jqre,jue->jqru", query_heads, piece[:, 0], preferred_element_type=jnp.float32)
        * scale
    )
    kept = key_pos[None, :] <= query_pos[:, None]
    scores = jnp.where(kept[None, None], scores, -1e30)
    new_top = jnp.maximum(top, jnp.max(scores, axis=-1))
    weights = jnp.where(kept[None, None], jnp.exp(scores - new_top[..., None]), 0.0)
    total = jnp.sum(weights, axis=-1)
    probs = weights.astype(jnp.bfloat16)
    acc = jnp.einsum("jqru,jue->jqre", probs, piece[:, 1], preferred_element_type=jnp.float32)
    top, total, acc = (new_top, total, acc)
    context = (acc / total[..., None]).astype(jnp.bfloat16)
    return jnp.transpose(context, (2, 0, 1, 3))


def solution(mesh):
    in_specs = (
        P("seq", "tp", "group", None),
        P("seq", ("group", "tp")),
        P(("group", "tp"), None, None, None),
        P(),
    )
    out_specs = P("seq", "tp", "group", None)
    return jax.shard_map(body, mesh=mesh, in_specs=in_specs, out_specs=out_specs, check_vma=False)
```

profile of v0, /device:TPU:1, one launch (start us, length us, event | category | flops | bytes accessed | tf_op | source)
XLA Modules:
  0.0 276.8 jit_solution(4109128155972550881)
XLA Ops:
  6.5 0.0 copy-start
  6.5 0.0 reduce-scatter.2.cloned.1.call-start
  6.5 2.3 reshape.134
  8.8 0.5 dot_general.14
  9.3 3.6 %convolution_bitcast_fusion = f32[8,2,512,128]{3,2,1,0:T(8,128)} fusion(bf16[8,2,128,160]{2,1,0,3:T(2,128)(2,1)S(1)} %dot_general.14, bf16[512,160]{0,1:T(8,128)(2,1)} %param.5), kind=kOutput, calls=%fused_computation.8 | convolution fusion | flops 335544320 | bytes 5013504 | tf_op jit(solution)/shard_map/dot_general | solution.py:20
  12.9 0.0 reduce-scatter.2.cloned.1.call-update
  12.9 0.0 all-gather.2.cloned.1.call-start
  12.9 136.3 %reduce-scatter.2.cloned.1.call-done = f32[1,2,512,128]{3,2,1,0:T(8,128)} async-done(((f32[8,2,512,128]{3,2,1,0:T(8,128)}), f32[1,2,512,128]{3,2,1,0:T(8,128)}) %reduce-scatter.2.cloned.1.call-update) | async-done | bytes 524304 | tf_op jit(solution)/shard_map/reduce_scatter | solution.py:25
  149.2 24.0 %all-reduce.1 = bf16[1,2,512,128]{3,2,1,0:T(8,128)(2,1)} all-reduce(f32[1,2,512,128]{3,2,1,0:T(8,128)} %reduce-scatter.2.cloned.1.call-done), channel_id=1, replica_groups=mesh['group'=4,'seq'=16,'tp'=8] {'group'}, use_global_device_ids=true, to_apply=%region_3.4 | all-reduce | flops 131072 | bytes 786432 | tf_op jit(solution)/shard_map/psum | solution.py:33
  173.2 0.0 all-gather.2.cloned.1.call-update
  173.3 0.7 select_reduce_fusion.1
  174.0 0.9 select_reduce_fusion
  175.0 3.9 %broadcast_compare_fusion = pred[512,8192]{0,1:T(8,128)(4,1)} fusion(s32[512]{0:T(512)S(1)} %fusion.27, s32[8192]{0:T(1024)S(1)} %fusion.25), kind=kLoop, calls=%fused_computation.7 | loop fusion | flops 4194304 | bytes 4229120 | tf_op jit(solution)/shard_map/le | solution.py:48
  178.9 40.4 %all-gather.2.cloned.1.call-done = bf16[1,2,8192,128]{3,2,1,0:T(8,128)(2,1)} async-done(((bf16[1,2,512,128]{3,2,1,0:T(8,128)(2,1)}), bf16[1,2,8192,128]{3,2,1,0:T(8,128)(2,1)}) %all-gather.2.cloned.1.call-update) | async-done | bytes 4194320 | tf_op jit(solution)/shard_map/all_gather | solution.py:40
  219.3 0.0 copy-done
  219.3 0.0 copy-start.1
  219.4 15.7 %fusion = (f32[2,512]{1,0:T(2,128)S(1)}, f32[8192,2,512]{2,0,1:T(8,128)}) fusion(pred[512,8192]{0,1:T(8,128)(4,1)} %broadcast_compare_fusion, bf16[2,512,128]{2,0,1:T(2,128)(2,1)S(1)} %bitcast.52, bf16[1,2,8192,128]{3,2,1,0:T(8,128)(2,1)} %all-gather.2.cloned.1.call-done), kind=kOutput, calls=%fused_computation.2 | convolution fusion | flops 2172648448 | bytes 40112128 | tf_op jit(solution)/shard_map/jqre,jue->jqru/dot_general | solution.py:45
  235.1 0.0 copy-done.1
  235.1 15.3 %fusion.1 = f32[2,512]{1,0:T(2,128)S(1)} fusion(f32[8192,2,512]{2,0,1:T(8,128)} %get-tuple-element.6, f32[2,512]{1,0:T(2,128)S(1)} %broadcast_maximum_fusion, pred[512,8192]{0,1:T(8,128)(4,1)S(1)} %copy-done.1), kind=kLoop, calls=%fused_computation.3 | loop fusion | flops 41942016 | bytes 37756928 | tf_op jit(solution)/shard_map/reduce_sum | solution.py:52
  250.4 18.6 %fusion.13 = bf16[512,1,2,128]{3,0,2,1:T(8,128)(2,1)S(1)} fusion(bf16[1,2,8192,128]{3,2,1,0:T(8,128)(2,1)} %all-gather.2.cloned.1.call-done, f32[8192,2,512]{2,0,1:T(8,128)} %get-tuple-element.6, f32[2,512]{1,0:T(2,128)S(1)} %broadcast_maximum_fusion, pred[512,8192]{0,1:T(8,128)(4,1)} %broadcast_compare_fusion, f32[2,512]{1,0:T(2,128)S(1)} %fusion.1), kind=kOutput, calls=%fused_computation.16 | convolution fusion | flops 2189688832 | bytes 40116224 | tf_op jit(solution)/shard_map/jqru,jue->jqre/dot_general | solution.py:54
  269.0 1.0 copy.15
  (5 shorter events, 0.0 us)
Async XLA Ops:
  6.5 212.8 %copy-start = (bf16[512,1,2,128]{3,2,1,0:T(2,128)(2,1)S(1)}, bf16[512,1,2,128]{3,2,1,0:T(2,128)(2,1)}, u32[]{:S(2)}) copy-start(bf16[512,1,2,128]{3,2,1,0:T(2,128)(2,1)} %param.4) | copy-start | bytes 786436
  6.5 142.7 %reduce-scatter.2.cloned.1.call-start = ((), (), s32[]{:S(2)}) async-start(), calls=%async_computation.1 | async-start | bytes 4718592 | tf_op jit(solution)/shard_map/reduce_scatter | solution.py:25
  12.9 206.4 %all-gather.2.cloned.1.call-start = ((), (), s32[]{:S(2)}) async-start(), calls=%async_computation.2 | async-start | bytes 4456448 | tf_op jit(solution)/shard_map/all_gather | solution.py:40
  219.3 15.7 %copy-start.1 = (pred[512,8192]{0,1:T(8,128)(4,1)S(1)}, pred[512,8192]{0,1:T(8,128)(4,1)}, u32[]{:S(2)}) copy-start(pred[512,8192]{0,1:T(8,128)(4,1)} %broadcast_compare_fusion) | copy-start | bytes 12582916
Sparse Core Ops, SparseCore 0:
  13.0 136.1 reduce-scatter.1
  173.4 45.9 all-gather.1
where the time goes:
time: 277 us
  waiting for transfers between devices  177 us (64%)
  matrix products  37.9 us (14%)
  blocking collectives  24 us (9%)
  other arithmetic  20.9 us (8%)
  between operations  13.5 us (5%)
  local copies, waits for them, and re-layouts  3.7 us (1%)
    reduce_scatter x1, waiting for transfers between devices, body(): lax.psum_scatter(jnp.transpose(part_sum.reshape(tok, kv_local * lax.axis_...  136 us
    all_gather x1, waiting for transfers between devices, body(): piece = lax.all_gather(key_values, 'seq', axis=2, tiled=True)  40.4 us
    psum x1, blocking collectives, body(): key_values = lax.psum(partial_kv, 'group').astype(jnp.bfloat16)  24 us
    dot_general x1, matrix products, body(): jnp.einsum('jqru,jue->jqre', probs, piece[:, 1], preferred_element_type=j...  18.6 us
    dot_general x1, matrix products, body(): jnp.einsum('jqre,jue->jqru', query_heads, piece[:, 0], preferred_element_...  15.7 us
    reduce_sum x1, other arithmetic, body(): total = jnp.sum(weights, axis=-1)  15.3 us
  transfers between devices with their start and end apart: 2, of which 2 were waited for; matrix products, arithmetic and copies ran while one was open for 2% of the time, Pallas kernels for 0%

commit v1 on v0

v1 whole, which is shorter than its diff:
```python
import functools

import jax
import jax.numpy as jnp
from jax import lax
from jax.experimental import pallas as pl
from jax.experimental.pallas import tpu as pltpu
from jax.sharding import PartitionSpec as P

MESH = pl.DeviceIdType.MESH
NX, NY, NZ, NG = 4, 8, 8, 4
QT = 128
ROWS = 256
NEG = -1e30
LOG2E = 1.4426950408889634


def kernel(
    order_ref,
    q_ref,
    aug_ref,
    w_ref,
    out_ref,
    augx,
    wx,
    op,
    om,
    ip,
    im,
    own,
    kvs,
    m_ref,
    l_ref,
    acc_ref,
    ax_s,
    ax_r,
    wx_s,
    wx_r,
    ws_s,
    ws_r,
    rp_s,
    rp_r,
    rm_s,
    rm_r,
    zg_s,
    zg_r,
    yp_s,
    yp_r,
    ym_s,
    ym_r,
    sb_s,
    sb_r,
    loc,
):
    g = lax.axis_index("group")
    seq = lax.axis_index("seq")
    tp = lax.axis_index("tp")
    y, c = lax.div(seq, 2), lax.rem(seq, 2)
    zh, x = lax.div(tp, NX), lax.rem(tp, NX)
    z = zh * NG + g

    def dev(z=z, y=y, c=c, x=x):
        return (lax.rem(z, NG), y * 2 + c, lax.div(z, NG) * NX + x)

    def remote(src, dst, send, recv, to):
        return pltpu.make_async_remote_copy(
            src_ref=src, dst_ref=dst, send_sem=send, recv_sem=recv, device_id=to, device_id_type=MESH
        )

    def wrap(v, n):
        return lax.rem(v + 4 * n, n)

    x_to = [dev(x=wrap(x + d, NX)) for d in (1, 2, 3)]
    z_next, z_prev = dev(z=wrap(z + 1, NZ)), dev(z=wrap(z - 1, NZ))
    g_to = [dev(z=zh * NG + wrap(g + d, NG)) for d in (1, 2, 3)]
    y_next, y_prev = dev(y=wrap(y + 1, NY)), dev(y=wrap(y - 1, NY))
    sib = dev(c=1 - c)

    barrier = pltpu.get_barrier_semaphore()
    partners = x_to + [z_next, z_prev] + g_to + [y_next, y_prev, sib]
    for to in partners:
        pl.semaphore_signal(barrier, inc=1, device_id=to, device_id_type=MESH)

    own_w = [
        pltpu.make_async_copy(w_ref.at[:, pl.ds(pl.multiple_of((x + NX * h) * 2 * QT, 2 * QT), 2 * QT)], wx.at[h, x], loc.at[h]) for h in (0, 1)
    ]
    own_a = [
        pltpu.make_async_copy(aug_ref.at[:, pl.ds(i * QT, QT)], augx.at[i, x], loc.at[2 + i])
        for i in range(NG)
    ]
    for cp in own_w + own_a:
        cp.start()
    pl.semaphore_wait(barrier, len(partners))

    w_sends = []
    for i, d in enumerate((1, 2, 3)):
        to_x = wrap(x + d, NX)
        cp = remote(w_ref.at[:, pl.ds(pl.multiple_of((to_x + NX * c) * 2 * QT, 2 * QT), 2 * QT)], wx.at[c, x], wx_s.at[i], wx_r.at[i], x_to[i])
        cp.start()
        w_sends.append(cp)
    quarters = [g, wrap(g - 1, NG), wrap(g + 1, NG), wrap(g + 2, NG)]
    a_sends = []
    for j, qt in enumerate(quarters):
        for i in range(3):
            cp = remote(
                aug_ref.at[:, pl.ds(pl.multiple_of(qt * QT, QT), QT)],
                augx.at[qt, x],
                ax_s.at[j, i],
                ax_r.at[j, i],
                x_to[i],
            )
            cp.start()
            a_sends.append(cp)
    w_shares = []
    for i, d in enumerate((1, 2, 3)):
        src = wrap(x - d, NX)
        remote(wx.at[c, src], wx.at[c, src], wx_s.at[i], wx_r.at[i], x_to[i]).wait_recv()
        cp = remote(wx.at[c, src], wx.at[c, src], ws_s.at[i], ws_r.at[i], sib)
        cp.start()
        w_shares.append(cp)
    for cp in own_w + own_a:
        cp.wait()
    for i, d in enumerate((1, 2, 3)):
        src = wrap(x - d, NX)
        remote(wx.at[1 - c, src], wx.at[1 - c, src], ws_s.at[i], ws_r.at[i], sib).wait_recv()

    def arrive_states(j):
        for i, d in enumerate((1, 2, 3)):
            slot = augx.at[quarters[j], wrap(x - d, NX)]
            remote(slot, slot, ax_s.at[j, i], ax_r.at[j, i], x_to[i]).wait_recv()

    def share(target):
        states = augx[lax.rem(target, NG)].reshape(NX * 160, QT)
        weights = wx[lax.div(target, NG)].reshape(NX * 160, 2 * QT)
        return lax.dot_general(
            states, weights, (((0,), (0,)), ((), ())), preferred_element_type=jnp.float32
        )

    sends = []

    def send_p(k, half):
        cp = remote(op.at[k - 1, half], ip.at[k - 1, half], rp_s.at[k - 1, half], rp_r.at[k - 1, half], z_next)
        cp.start()
        sends.append(cp)

    def send_m(k, half):
        cp = remote(om.at[k - 1, half], im.at[k - 1, half], rm_s.at[k - 1, half], rm_r.at[k - 1, half], z_prev)
        cp.start()
        sends.append(cp)

    def got_p(k, half):
        slot = ip.at[k - 1, half]
        remote(slot, slot, rp_s.at[k - 1, half], rp_r.at[k - 1, half], z_next).wait_recv()
        return ip[k - 1, half]

    def got_m(k, half):
        slot = im.at[k - 1, half]
        remote(slot, slot, rm_s.at[k - 1, half], rm_r.at[k - 1, half], z_prev).wait_recv()
        return im[k - 1, half]

    arrive_states(0)
    part = share(wrap(z + 4, NZ))
    op[3, 0] = part[:, :QT]
    om[3, 1] = part[:, QT:]
    send_p(4, 0)
    send_m(4, 1)
    arrive_states(1)
    part = share(wrap(z + 3, NZ))
    op[2, 1] = part[:, QT:]
    send_p(3, 1)
    op[2, 0] = part[:, :QT]
    arrive_states(2)
    part = share(wrap(z - 3, NZ))
    om[2, 0] = part[:, :QT]
    send_m(3, 0)
    om[2, 1] = part[:, QT:]
    arrive_states(3)
    part = share(wrap(z + 2, NZ))
    op[1, 0] = part[:, :QT]
    op[1, 1] = part[:, QT:]
    part = share(wrap(z - 2, NZ))
    om[1, 0] = part[:, :QT]
    om[1, 1] = part[:, QT:]
    op[2, 0] += got_p(4, 0)
    send_p(3, 0)
    om[2, 1] += got_m(4, 1)
    send_m(3, 1)
    part = share(wrap(z + 1, NZ))
    op[0, 0] = part[:, :QT]
    op[0, 1] = part[:, QT:]
    part = share(wrap(z - 1, NZ))
    om[0, 0] = part[:, :QT]
    om[0, 1] = part[:, QT:]
    own[...] = share(z)
    for k in (3, 2):
        for first in (0, 1):
            hp, hm = 1 - first, first
            op[k - 2, hp] += got_p(k, hp)
            send_p(k - 1, hp)
            om[k - 2, hm] += got_m(k, hm)
            send_m(k - 1, hm)

    low = own[:, :QT] + got_m(1, 0)
    high = own[:, QT:] + got_p(1, 1)
    low += got_p(1, 0)
    high += got_m(1, 1)
    kvs[y, c, g, :, :QT] = low.astype(jnp.bfloat16)
    kvs[y, c, g, :, QT:] = high.astype(jnp.bfloat16)

    for i in range(3):
        slot = kvs.at[y, c, g]
        cp = remote(slot, slot, zg_s.at[i], zg_r.at[i], g_to[i])
        cp.start()
        sends.append(cp)

    def ring_p(d, qi, qt):
        slot = kvs.at[wrap(y - d, NY), c, qt]
        return remote(slot, slot, yp_s.at[d, qi], yp_r.at[d, qi], y_next)

    def ring_m(d, qi, qt):
        slot = kvs.at[wrap(y + d, NY), c, qt]
        return remote(slot, slot, ym_s.at[d, qi], ym_r.at[d, qi], y_prev)

    for i in range(NG):
        qt = wrap(g - i, NG)
        if i > 0:
            slot = kvs.at[y, c, qt]
            remote(slot, slot, zg_s.at[i - 1], zg_r.at[i - 1], g_to[i - 1]).wait_recv()
        ring_p(0, qt, qt).start()
        ring_m(0, qt, qt).start()

    def sibling(yi, ci, idx):
        slot = kvs.at[yi, ci]
        return remote(slot, slot, sb_s.at[idx], sb_r.at[idx], sib)

    sibling(y, c, y).start()

    scale = LOG2E * 128 ** -0.5

    def attend(yi, ci, diagonal=False):
        def rows_of(rb, carry):
            base = pl.multiple_of(rb * ROWS, ROWS)
            a = lax.div(rb, 512 // ROWS)
            qo = order_ref[2 * seq + a]
            q = q_ref[pl.ds(base, ROWS), :]
            block = kvs.at[yi, ci].reshape(4 * QT, 2 * QT)
            keys = block[:, :QT]
            values = block[:, QT:]
            s = lax.dot_general(q, keys, (((1,), (1,)), ((), ())), preferred_element_type=jnp.float32)
            if diagonal:
                row = lax.broadcasted_iota(jnp.int32, (ROWS, 256), 0) + lax.rem(rb, 512 // ROWS) * ROWS
                row = lax.shift_right_logical(row, 1)
                col = lax.broadcasted_iota(jnp.int32, (ROWS, 256), 1)
                parts = []
                for h in (0, 1):
                    ko = order_ref[2 * (yi * 2 + ci) + h]
                    kept = ko * 256 + col <= qo * 256 + row
                    parts.append(jnp.where(kept, s[:, h * 256 : (h + 1) * 256], NEG))
                top = jnp.max(jnp.maximum(parts[0], parts[1]), axis=-1, keepdims=True)
                new = top
                shifted = [(p - new) * scale for p in parts]
            else:
                old = m_ref[pl.ds(base, ROWS), :]
                parts = [s[:, h * 256 : (h + 1) * 256] for h in (0, 1)]
                new = old[:, :1]
                bias = []
                for h in (0, 1):
                    ko = order_ref[2 * (yi * 2 + ci) + h]
                    b = jnp.where(ko < qo, 0.0, NEG)
                    bias.append(b)
                    new = jnp.maximum(new, jnp.max(parts[h], axis=-1, keepdims=True) + b)
                shifted = [(parts[h] - (new - bias[h])) * scale for h in (0, 1)]
            p = [jnp.exp2(v) for v in shifted]
            total = p[0][:, :128] + p[0][:, 128:] + p[1][:, :128] + p[1][:, 128:]
            probs = jnp.concatenate([v.astype(jnp.bfloat16) for v in p], axis=1)
            o = jnp.dot(probs, values, preferred_element_type=jnp.float32)
            if diagonal:
                l_ref[pl.ds(base, ROWS), :] = total
                acc_ref[pl.ds(base, ROWS), :] = o
            else:
                alpha = jnp.exp2((old[:, :1] - new) * scale)
                l_ref[pl.ds(base, ROWS), :] = l_ref[pl.ds(base, ROWS), :] * alpha + total
                acc_ref[pl.ds(base, ROWS), :] = acc_ref[pl.ds(base, ROWS), :] * alpha + o
            m_ref[pl.ds(base, ROWS), :] = jnp.broadcast_to(new, (ROWS, 128))
            return carry

        lax.fori_loop(0, 1024 // ROWS, rows_of, 0)

    attend(y, c, True)

    def wait_sibling(yi):
        sibling(yi, 1 - c, yi).wait_recv()

    def step(d, carry):
        last_p, last_m = wrap(y - d + 1, NY), wrap(y + d - 1, NY)
        new_p, new_m = wrap(y - d, NY), wrap(y + d, NY)
        for qt in range(NG):
            ring_p_slot = kvs.at[new_p, c, qt]
            ring_m_slot = kvs.at[new_m, c, qt]
            remote(ring_p_slot, ring_p_slot, yp_s.at[d - 1, qt], yp_r.at[d - 1, qt], y_next).wait_recv()

            @pl.when((d < 3) | (qt < 2))
            def _():
                ring_p(d, qt, qt).start()

            remote(ring_m_slot, ring_m_slot, ym_s.at[d - 1, qt], ym_r.at[d - 1, qt], y_prev).wait_recv()

            @pl.when((d < 3) | (qt >= 2))
            def _():
                ring_m(d, qt, qt).start()

            if qt == 0:

                @pl.when(d > 1)
                def _():
                    attend(last_p, c)

            elif qt == 1:

                @pl.when(d > 1)
                def _():
                    attend(last_m, c)

            elif qt == 2:
                wait_sibling(last_p)
                attend(last_p, 1 - c)
            else:

                @pl.when(d > 1)
                def _():
                    wait_sibling(last_m)
                    attend(last_m, 1 - c)

        sibling(new_p, c, new_p).start()
        sibling(new_m, c, new_m).start()
        return carry

    lax.fori_loop(1, 4, step, 0)
    far = wrap(y + 4, NY)
    for n, (qp, qm) in enumerate(((0, 2), (1, 3))):
        slot = kvs.at[far, c, qp]
        remote(slot, slot, yp_s.at[3, qp], yp_r.at[3, qp], y_next).wait_recv()
        slot = kvs.at[far, c, qm]
        remote(slot, slot, ym_s.at[3, qm], ym_r.at[3, qm], y_prev).wait_recv()
        if n == 0:
            attend(wrap(y - 3, NY), c)
            attend(wrap(y + 3, NY), c)
    sibling(far, c, far).start()
    wait_sibling(wrap(y - 3, NY))
    attend(wrap(y - 3, NY), 1 - c)
    wait_sibling(wrap(y + 3, NY))
    attend(wrap(y + 3, NY), 1 - c)
    attend(far, c)
    wait_sibling(far)
    attend(far, 1 - c)

    total = jnp.sum(l_ref[...], axis=-1, keepdims=True)
    out_ref[...] = (acc_ref[...] / total).astype(jnp.bfloat16)

    for cp in w_sends + a_sends + w_shares + sends:
        cp.wait_send()

    def drain(d, carry):
        for qt in range(NG):

            @pl.when((d < 3) | (qt < 2))
            def _():
                ring_p(d, qt, qt).wait_send()

            @pl.when((d < 3) | (qt >= 2))
            def _():
                ring_m(d, qt, qt).wait_send()

        return carry

    lax.fori_loop(0, 4, drain, 0)

    def drain_sibling(yi, carry):
        sibling(yi, c, yi).wait_send()
        return carry

    lax.fori_loop(0, NY, drain_sibling, 0)


def body(queries, aug_states, key_value_weight, block_order):
    tok = queries.shape[0]
    rows = tok * queries.shape[2]
    q = queries.reshape(rows, 128)
    aug = aug_states.T
    w = key_value_weight.reshape(160, 2048)
    dma = pltpu.SemaphoreType.DMA
    out = pl.pallas_call(
        kernel,
        out_shape=jax.ShapeDtypeStruct((rows, 128), jnp.bfloat16),
        in_specs=[pl.BlockSpec(memory_space=pltpu.SMEM)] + [pl.BlockSpec(memory_space=pltpu.VMEM)] * 3,
        out_specs=pl.BlockSpec(memory_space=pltpu.VMEM),
        scratch_shapes=[
            pltpu.VMEM((NG, NX, 160, QT), jnp.bfloat16),
            pltpu.VMEM((2, NX, 160, 2 * QT), jnp.bfloat16),
            pltpu.VMEM((4, 2, QT, QT), jnp.float32),
            pltpu.VMEM((4, 2, QT, QT), jnp.float32),
            pltpu.VMEM((4, 2, QT, QT), jnp.float32),
            pltpu.VMEM((4, 2, QT, QT), jnp.float32),
            pltpu.VMEM((QT, 2 * QT), jnp.float32),
            pltpu.VMEM((NY, 2, NG, QT, 2 * QT), jnp.bfloat16),
            pltpu.VMEM((rows, 128), jnp.float32),
            pltpu.VMEM((rows, 128), jnp.float32),
            pltpu.VMEM((rows, 128), jnp.float32),
            dma((4, 3)),
            dma((4, 3)),
            dma((3,)),
            dma((3,)),
            dma((3,)),
            dma((3,)),
            dma((4, 2)),
            dma((4, 2)),
            dma((4, 2)),
            dma((4, 2)),
            dma((3,)),
            dma((3,)),
            dma((4, 4)),
            dma((4, 4)),
            dma((4, 4)),
            dma((4, 4)),
            dma((8,)),
            dma((8,)),
            dma((6,)),
        ],
        compiler_params=pltpu.CompilerParams(
            collective_id=0, has_side_effects=True, vmem_limit_bytes=40 * 1024 * 1024
        ),
        cost_estimate=pl.CostEstimate(flops=9 * 10**9, bytes_accessed=2 * 10**6, transcendentals=8 * 10**6),
        name="compose",
    )(block_order, q, aug, w)
    return out.reshape(queries.shape)


def solution(mesh):
    in_specs = (
        P("seq", "tp", "group", None),
        P("seq", ("group", "tp")),
        P(("group", "tp"), None, None, None),
        P(),
    )
    out_specs = P("seq", "tp", "group", None)
    return jax.shard_map(body, mesh=mesh, in_specs=in_specs, out_specs=out_specs, check_vma=False)
```

time: 277 us -> 86.1 us (0.31)
  waiting for transfers between devices: 177 us -> 0 us
  Pallas kernels: 0 us -> 81.8 us
  matrix products: 37.9 us -> 0 us
  blocking collectives: 24 us -> 0 us
  other arithmetic: 20.9 us -> 0 us
  between operations: 13.5 us -> 0.04 us
    reduce_scatter x1 -> x0, waiting for transfers between devices: 136 us -> none  [body(): lax.psum_scatter(jnp.transpose(part_sum.reshape(tok, kv_local * lax.axis_...]
    pallas_call x0 -> x1, Pallas kernels: none -> 81.8 us  [body(): pl.pallas_call(kernel, out_shape=jax.ShapeDtypeStruct((rows, 128), jnp.bf...]
    all_gather x1 -> x0, waiting for transfers between devices: 40.4 us -> none  [body(): piece = lax.all_gather(key_values, 'seq', axis=2, tiled=True)]
    dot_general x3 -> x0, matrix products: 37.9 us -> none  [the longest x1 18.6 us: body(): jnp.einsum('jqru,jue->jqre', probs, piece[:, 1], preferred_element_type=j...]
    psum x1 -> x0, blocking collectives: 24 us -> none  [body(): key_values = lax.psum(partial_kv, 'group').astype(jnp.bfloat16)]
    reduce_sum x3 -> x0, other arithmetic: 17 us -> none  [the longest x1 15.3 us: body(): total = jnp.sum(weights, axis=-1)]
    le x1 -> x0, other arithmetic: 3.93 us -> none  [body(): kept = key_pos[None, :] <= query_pos[:, None]]
  transfers between devices with their start and end apart: 2 -> 0, of which waited for: 2 -> 0; matrix products, arithmetic and copies ran while one was open for 2% -> 0% of each run, Pallas kernels for 0% -> 0%
where the time goes in v1:
time: 86.1 us; the launch traced here: 84.8 us
  Pallas kernels  81.8 us (95%)
  local copies, waits for them, and re-layouts  2.99 us (3%)
    pallas_call x1, Pallas kernels, body(): pl.pallas_call(kernel, out_shape=jax.ShapeDtypeStruct((rows, 128), jnp.bf...  81.8 us
    reshape x1, local copies, waits for them, and re-layouts, body(): w = key_value_weight.reshape(160, 2048)  2.27 us

profile of v1, /device:TPU:1, one launch (start us, length us, event | category | flops | bytes accessed | tf_op | source)
XLA Modules:
  0.0 84.8 jit_solution(15904363408354726199)
XLA Ops:
  0.0 0.0 copy-start
  0.0 0.0 copy-start.1
  0.0 0.0 copy-start.2
  0.0 2.3 %reshape.10.w_ref = bf16[160,2048]{1,0:T(8,128)(2,1)S(1)} reshape(bf16[160,8,2,128]{3,2,1,0:T(2,128)(2,1)} %param.6) | data formatting | bytes 1310720 | tf_op jit(solution)/shard_map/reshape | solution.py:390
  2.3 0.0 copy-done
  2.3 0.0 copy-done.1
  2.3 0.0 copy-done.2
  2.3 81.8 %compose.1 = bf16[1024,128]{1,0:T(8,128)(2,1)S(1)} custom-call(s32[32]{0:T(128)S(1)} %copy-done.2, bf16[1024,128]{1,0:T(8,128)(2,1)S(1)} %bitcast.6, bf16[160,512]{1,0:T(8,128)(2,1)S(1)} %bitcast.7, bf16[160,2048]{1,0:T(8,128)(2,1)S(1)} %reshape.10.w_ref), custom_call_target="tpu_custom_call" | custom-call | flops 8999999488 | bytes 2000000 | tf_op jit(solution)/shard_map/compose/pallas_call | solution.py:392
  84.1 0.7 copy.7
Async XLA Ops:
  0.0 2.3 %copy-start = (bf16[512,1,2,128]{3,2,1,0:T(2,128)(2,1)S(1)}, bf16[512,1,2,128]{3,2,1,0:T(2,128)(2,1)}, u32[]{:S(2)}) copy-start(bf16[512,1,2,128]{3,2,1,0:T(2,128)(2,1)} %param.4) | copy-start | bytes 786436
  0.0 2.3 %copy-start.1 = (bf16[512,160]{0,1:T(8,128)(2,1)S(1)}, bf16[512,160]{0,1:T(8,128)(2,1)}, u32[]{:S(2)}) copy-start(bf16[512,160]{0,1:T(8,128)(2,1)} %param.5) | copy-start | bytes 491524
  0.0 2.3 %copy-start.2 = (s32[32]{0:T(128)S(1)}, s32[32]{0:T(128)}, u32[]{:S(2)}) copy-start(s32[32]{0:T(128)} %order_ref.1) | copy-start | bytes 388

commit v2 on v1

v2 whole, which is shorter than its diff:
```python
import functools

import jax
import jax.numpy as jnp
from jax import lax
from jax.experimental import pallas as pl
from jax.experimental.pallas import tpu as pltpu
from jax.sharding import PartitionSpec as P

MESH = pl.DeviceIdType.MESH
NX, NY, NZ, NG = 4, 8, 8, 4
QT = 128
ROWS = 256
NEG = -1e30
LOG2E = 1.4426950408889634


def kernel(
    order_ref,
    q_hbm,
    aug_hbm,
    w_hbm,
    out_ref,
    q_ref,
    aug_ref,
    w_ref,
    w_wide,
    w_heads,
    augx,
    wx,
    op,
    om,
    ip,
    im,
    own,
    kvs,
    m_ref,
    l_ref,
    acc_ref,
    sc0,
    sc1,
    ax_s,
    ax_r,
    wx_s,
    wx_r,
    ws_s,
    ws_r,
    rp_s,
    rp_r,
    rm_s,
    rm_r,
    zg_s,
    zg_r,
    zq_s,
    zq_r,
    yp_s,
    yp_r,
    ym_s,
    ym_r,
    sb_s,
    sb_r,
    loc,
):
    g = lax.axis_index("group")
    seq = lax.axis_index("seq")
    tp = lax.axis_index("tp")
    y, c = lax.div(seq, 2), lax.rem(seq, 2)
    zh, x = lax.div(tp, NX), lax.rem(tp, NX)
    z = zh * NG + g

    def dev(z=z, y=y, c=c, x=x):
        return (lax.rem(z, NG), y * 2 + c, lax.div(z, NG) * NX + x)

    def remote(src, dst, send, recv, to):
        return pltpu.make_async_remote_copy(
            src_ref=src, dst_ref=dst, send_sem=send, recv_sem=recv, device_id=to, device_id_type=MESH
        )

    def wrap(v, n):
        return lax.rem(v + 4 * n, n)

    x_to = [dev(x=wrap(x + d, NX)) for d in (1, 2, 3)]
    z_next, z_prev = dev(z=wrap(z + 1, NZ)), dev(z=wrap(z - 1, NZ))
    g1, g2, g3 = g + 1 - 2 * lax.rem(g, 2), lax.rem(g + 2, NG), 3 - g
    g_to = [dev(z=zh * NG + v) for v in (g1, g2, g3)]
    y_next, y_prev = dev(y=wrap(y + 1, NY)), dev(y=wrap(y - 1, NY))
    sib = dev(c=1 - c)

    barrier = pltpu.get_barrier_semaphore()
    partners = x_to + [z_next, z_prev] + g_to + [y_next, y_prev, sib]
    for to in partners:
        pl.semaphore_signal(barrier, inc=1, device_id=to, device_id_type=MESH)

    loads = [
        pltpu.make_async_copy(w_hbm, w_ref, loc.at[0]),
        pltpu.make_async_copy(aug_hbm, aug_ref, loc.at[1]),
        pltpu.make_async_copy(q_hbm, q_ref, loc.at[2]),
    ]
    for cp in loads:
        cp.start()
    loads[0].wait()
    w_wide[...] = w_ref[...].astype(jnp.float32)
    for j in range(8):
        for half in (0, 1):
            w_heads[j, :, half * QT : (half + 1) * QT] = w_wide[pl.ds(2 * j + half, 160, stride=16), :].astype(
                jnp.bfloat16
            )
    for h in (0, 1):
        wx[h, x] = w_heads[x + NX * h]
    loads[1].wait()
    for i in range(NG):
        augx[i, x] = aug_ref[:, i * QT : (i + 1) * QT]
    pl.semaphore_wait(barrier, len(partners))

    w_sends = []
    for i, d in enumerate((1, 2, 3)):
        to_x = wrap(x + d, NX)
        cp = remote(w_heads.at[to_x + NX * c], wx.at[c, x], wx_s.at[i], wx_r.at[i], x_to[i])
        cp.start()
        w_sends.append(cp)
    quarters = [g, wrap(g - 1, NG), wrap(g + 1, NG), wrap(g + 2, NG)]
    a_sends = []
    for j, qt in enumerate(quarters):
        for i in range(3):
            cp = remote(
                augx.at[qt, x],
                augx.at[qt, x],
                ax_s.at[j, i],
                ax_r.at[j, i],
                x_to[i],
            )
            cp.start()
            a_sends.append(cp)
    w_shares = []
    for i, d in enumerate((1, 2, 3)):
        src = wrap(x - d, NX)
        remote(wx.at[c, src], wx.at[c, src], wx_s.at[i], wx_r.at[i], x_to[i]).wait_recv()
        cp = remote(wx.at[c, src], wx.at[c, src], ws_s.at[i], ws_r.at[i], sib)
        cp.start()
        w_shares.append(cp)
    for i, d in enumerate((1, 2, 3)):
        src = wrap(x - d, NX)
        remote(wx.at[1 - c, src], wx.at[1 - c, src], ws_s.at[i], ws_r.at[i], sib).wait_recv()

    def arrive_states(j):
        for i, d in enumerate((1, 2, 3)):
            slot = augx.at[quarters[j], wrap(x - d, NX)]
            remote(slot, slot, ax_s.at[j, i], ax_r.at[j, i], x_to[i]).wait_recv()

    def share(target):
        states = augx[lax.rem(target, NG)].reshape(NX * 160, QT)
        weights = wx[lax.div(target, NG)].reshape(NX * 160, 2 * QT)
        return lax.dot_general(
            states, weights, (((0,), (0,)), ((), ())), preferred_element_type=jnp.float32
        )

    sends = []

    def send_p(k, half):
        cp = remote(op.at[k - 1, half], ip.at[k - 1, half], rp_s.at[k - 1, half], rp_r.at[k - 1, half], z_next)
        cp.start()
        sends.append(cp)

    def send_m(k, half):
        cp = remote(om.at[k - 1, half], im.at[k - 1, half], rm_s.at[k - 1, half], rm_r.at[k - 1, half], z_prev)
        cp.start()
        sends.append(cp)

    def got_p(k, half):
        slot = ip.at[k - 1, half]
        remote(slot, slot, rp_s.at[k - 1, half], rp_r.at[k - 1, half], z_next).wait_recv()
        return ip[k - 1, half]

    def got_m(k, half):
        slot = im.at[k - 1, half]
        remote(slot, slot, rm_s.at[k - 1, half], rm_r.at[k - 1, half], z_prev).wait_recv()
        return im[k - 1, half]

    arrive_states(0)
    part = share(wrap(z + 4, NZ))
    op[3, 0] = part[:, :QT]
    om[3, 1] = part[:, QT:]
    send_p(4, 0)
    send_m(4, 1)
    arrive_states(1)
    part = share(wrap(z + 3, NZ))
    op[2, 1] = part[:, QT:]
    send_p(3, 1)
    op[2, 0] = part[:, :QT]
    arrive_states(2)
    part = share(wrap(z - 3, NZ))
    om[2, 0] = part[:, :QT]
    send_m(3, 0)
    om[2, 1] = part[:, QT:]
    arrive_states(3)
    part = share(wrap(z + 2, NZ))
    op[1, 0] = part[:, :QT]
    op[1, 1] = part[:, QT:]
    part = share(wrap(z - 2, NZ))
    om[1, 0] = part[:, :QT]
    om[1, 1] = part[:, QT:]
    op[2, 0] += got_p(4, 0)
    send_p(3, 0)
    om[2, 1] += got_m(4, 1)
    send_m(3, 1)
    part = share(wrap(z + 1, NZ))
    op[0, 0] = part[:, :QT]
    op[0, 1] = part[:, QT:]
    part = share(wrap(z - 1, NZ))
    om[0, 0] = part[:, :QT]
    om[0, 1] = part[:, QT:]
    own[...] = share(z)
    for k in (3, 2):
        for first in (0, 1):
            hp, hm = 1 - first, first
            op[k - 2, hp] += got_p(k, hp)
            send_p(k - 1, hp)
            om[k - 2, hm] += got_m(k, hm)
            send_m(k - 1, hm)

    low = own[:, :QT] + got_m(1, 0)
    high = own[:, QT:] + got_p(1, 1)
    low += got_p(1, 0)
    high += got_m(1, 1)
    kvs[y, c, g, :, :QT] = low.astype(jnp.bfloat16)
    kvs[y, c, g, :, QT:] = high.astype(jnp.bfloat16)

    def quarter_of_own(e, qt):
        slot = kvs.at[y, c, qt]
        return remote(slot, slot, zg_s.at[e - 1], zg_r.at[e - 1], g_to[e - 1])

    for e in (2, 3, 1):
        cp = quarter_of_own(e, g)
        cp.start()
        sends.append(cp)

    units = (g, g2, g3)

    def ring_p(d, u):
        slot = kvs.at[wrap(y - d, NY), c, units[u]]
        return remote(slot, slot, yp_s.at[d, u], yp_r.at[d, u], y_next)

    def ring_m(d, u):
        slot = kvs.at[wrap(y + d, NY), c, units[u]]
        return remote(slot, slot, ym_s.at[d, u], ym_r.at[d, u], y_prev)

    def arrive_p(d, u):
        slot = kvs.at[wrap(y - d, NY), c, units[u]]
        remote(slot, slot, yp_s.at[d - 1, u], yp_r.at[d - 1, u], y_next).wait_recv()

    def arrive_m(d, u):
        slot = kvs.at[wrap(y + d, NY), c, units[u]]
        remote(slot, slot, ym_s.at[d - 1, u], ym_r.at[d - 1, u], y_prev).wait_recv()

    def swap_p(d, qt):
        slot = kvs.at[wrap(y - d, NY), c, qt]
        return remote(slot, slot, zq_s.at[d - 1], zq_r.at[d - 1], g_to[0])

    def swap_m(d, qt):
        slot = kvs.at[wrap(y + d, NY), c, lax.rem(qt + 2 * lax.div(d, 4), NG)]
        return remote(slot, slot, zq_s.at[3 + d], zq_r.at[3 + d], g_to[0])

    def sibling(yi, ci):
        slot = kvs.at[yi, ci]
        return remote(slot, slot, sb_s.at[yi], sb_r.at[yi], sib)

    for u in range(3):
        if u > 0:
            quarter_of_own(u + 1, units[u]).wait_recv()
        ring_p(0, u).start()
        ring_m(0, u).start()
    quarter_of_own(1, g1).wait_recv()
    sibling(y, c).start()
    loads[2].wait()

    scale = LOG2E * 128 ** -0.5
    scores = (sc0, sc1)

    def score(yi, rb):
        q = q_ref[rb * ROWS : (rb + 1) * ROWS, :]
        block = kvs.at[yi].reshape(8 * QT, 2 * QT)
        for h in range(4):
            scores[rb % 2][:, h * 256 : (h + 1) * 256] = lax.dot_general(
                q, block[h * 256 : (h + 1) * 256, :QT], (((1,), (1,)), ((), ())), preferred_element_type=jnp.float32
            )

    def weigh(yi, rb, diagonal):
        rows = slice(rb * ROWS, (rb + 1) * ROWS)
        block = kvs.at[yi].reshape(8 * QT, 2 * QT)
        qo = order_ref[2 * seq + rb * ROWS // 512]
        s = scores[rb % 2]
        parts = [s[:, i * QT : (i + 1) * QT] for i in range(8)]
        if diagonal:
            row = lax.broadcasted_iota(jnp.int32, (ROWS, QT), 0) + (rb * ROWS) % 512
            ahead = lax.shift_right_logical(row, 1) - lax.broadcasted_iota(jnp.int32, (ROWS, QT), 1)
            for i in range(8):
                ko = order_ref[4 * yi + i // 2]
                parts[i] = jnp.where(ahead >= (ko - qo) * 256 + (i % 2) * QT, parts[i], NEG)
            bias = [None] * 4
        else:
            bias = [jnp.where(order_ref[4 * yi + h] < qo, 0.0, NEG) for h in range(4)]
        top = None
        for h in range(4):
            t = jnp.maximum(parts[2 * h], parts[2 * h + 1])
            t = t if diagonal else t + bias[h]
            top = t if top is None else jnp.maximum(top, t)
        new = jnp.broadcast_to(jnp.max(top, axis=-1, keepdims=True), (ROWS, QT))
        if not diagonal:
            old = m_ref[rows, :]
            new = jnp.maximum(old, new)
        m_ref[rows, :] = new
        total, o = None, None
        for h in range(4):
            base = new if diagonal else new - bias[h]
            pair = [jnp.exp2((parts[2 * h + i] - base) * scale) for i in (0, 1)]
            t = pair[0] + pair[1]
            total = t if total is None else total + t
            probs = jnp.concatenate([v.astype(jnp.bfloat16) for v in pair], axis=1)
            t = jnp.dot(probs, block[h * 256 : (h + 1) * 256, QT:], preferred_element_type=jnp.float32)
            o = t if o is None else o + t
        if diagonal:
            l_ref[rows, :] = total
            acc_ref[rows, :] = o
        else:
            alpha = jnp.exp2((old - new) * scale)
            l_ref[rows, :] = l_ref[rows, :] * alpha + total
            acc_ref[rows, :] = acc_ref[rows, :] * alpha + o

    def first_half(yi, diagonal=False):
        score(yi, 0)
        score(yi, 1)
        weigh(yi, 0, diagonal)
        score(yi, 2)
        weigh(yi, 1, diagonal)

    def second_half(yi, diagonal=False):
        score(yi, 3)
        weigh(yi, 2, diagonal)
        weigh(yi, 3, diagonal)

    def when(cond, do):
        if isinstance(cond, bool):
            if cond:
                do()
        else:
            pl.when(cond)(do)

    def step(d):
        new_p, new_m = wrap(y - d, NY), wrap(y + d, NY)

        def unit(u):
            def plus():
                arrive_p(d, u)
                when(d < 4 if u == 0 else d < 3, lambda: ring_p(d, u).start())
                if u == 0:
                    swap_p(d, g).start()

            def minus():
                arrive_m(d, u)
                when(d < 4 if u == 1 else d < 3, lambda: ring_m(d, u).start())
                if u == 0:
                    swap_m(d, g).start()
                elif u == 1:
                    when(d == 4, lambda: swap_m(d, g).start())

            when(True if u == 0 else d < 4, plus)
            when(True if u == 1 else d < 4, minus)

        def complete():
            swap_p(d, g1).wait_recv()
            swap_m(d, g1).wait_recv()
            sibling(new_p, c).start()
            when(d < 4, lambda: sibling(new_m, c).start())

        return unit, complete

    def wait_sibling(yi):
        sibling(yi, 1 - c).wait_recv()

    unit, complete = step(1)
    wait_sibling(y)
    first_half(y, True)
    unit(0)
    second_half(y, True)
    unit(1)
    unit(2)
    complete()

    def onward(d, carry):
        unit, complete = step(d)
        last_p, last_m = wrap(y - d + 1, NY), wrap(y + d - 1, NY)
        unit(0)
        wait_sibling(last_p)
        first_half(last_p)
        unit(1)
        wait_sibling(last_m)
        second_half(last_p)
        first_half(last_m)
        unit(2)
        complete()
        second_half(last_m)
        return carry

    lax.fori_loop(2, 5, onward, 0)
    far = wrap(y + 4, NY)
    wait_sibling(far)
    first_half(far)
    second_half(far)

    out_ref[...] = (acc_ref[...] / jnp.sum(l_ref[...], axis=-1, keepdims=True)).astype(jnp.bfloat16)

    for cp in w_sends + a_sends + w_shares + sends:
        cp.wait_send()

    def drain(d, carry):
        for u in range(3):
            when(True if u == 0 else d < 3, lambda: ring_p(d, u).wait_send())
            when(True if u == 1 else d < 3, lambda: ring_m(d, u).wait_send())
        swap_p(d + 1, g).wait_send()
        swap_m(d + 1, g).wait_send()
        return carry

    lax.fori_loop(0, 4, drain, 0)

    def drain_sibling(yi, carry):
        sibling(yi, c).wait_send()
        return carry

    lax.fori_loop(0, NY, drain_sibling, 0)


def body(queries, aug_states, key_value_weight, block_order):
    tok = queries.shape[0]
    rows = tok * queries.shape[2]
    q = queries.reshape(rows, 128)
    aug = aug_states.T
    w = key_value_weight.reshape(2560, 128)
    dma = pltpu.SemaphoreType.DMA
    out = pl.pallas_call(
        kernel,
        out_shape=jax.ShapeDtypeStruct((rows, 128), jnp.bfloat16),
        in_specs=[pl.BlockSpec(memory_space=pltpu.SMEM)] + [pl.BlockSpec(memory_space=pltpu.HBM)] * 3,
        out_specs=pl.BlockSpec(memory_space=pltpu.VMEM),
        scratch_shapes=[
            pltpu.VMEM((rows, 128), jnp.bfloat16),
            pltpu.VMEM((160, 512), jnp.bfloat16),
            pltpu.VMEM((2560, 128), jnp.bfloat16),
            pltpu.VMEM((2560, 128), jnp.float32),
            pltpu.VMEM((8, 160, 2 * QT), jnp.bfloat16),
            pltpu.VMEM((NG, NX, 160, QT), jnp.bfloat16),
            pltpu.VMEM((2, NX, 160, 2 * QT), jnp.bfloat16),
            pltpu.VMEM((4, 2, QT, QT), jnp.float32),
            pltpu.VMEM((4, 2, QT, QT), jnp.float32),
            pltpu.VMEM((4, 2, QT, QT), jnp.float32),
            pltpu.VMEM((4, 2, QT, QT), jnp.float32),
            pltpu.VMEM((QT, 2 * QT), jnp.float32),
            pltpu.VMEM((NY, 2, NG, QT, 2 * QT), jnp.bfloat16),
            pltpu.VMEM((rows, 128), jnp.float32),
            pltpu.VMEM((rows, 128), jnp.float32),
            pltpu.VMEM((rows, 128), jnp.float32),
            pltpu.VMEM((ROWS, 8 * QT), jnp.float32),
            pltpu.VMEM((ROWS, 8 * QT), jnp.float32),
            dma((4, 3)),
            dma((4, 3)),
            dma((3,)),
            dma((3,)),
            dma((3,)),
            dma((3,)),
            dma((4, 2)),
            dma((4, 2)),
            dma((4, 2)),
            dma((4, 2)),
            dma((3,)),
            dma((3,)),
            dma((8,)),
            dma((8,)),
            dma((4, 3)),
            dma((4, 3)),
            dma((4, 3)),
            dma((4, 3)),
            dma((8,)),
            dma((8,)),
            dma((6,)),
        ],
        compiler_params=pltpu.CompilerParams(
            collective_id=0, has_side_effects=True, vmem_limit_bytes=62 * 1024 * 1024
        ),
        cost_estimate=pl.CostEstimate(flops=9 * 10**9, bytes_accessed=2 * 10**6, transcendentals=8 * 10**6),
        name="compose",
    )(block_order, q, aug, w)
    return out.reshape(queries.shape)


def solution(mesh):
    in_specs = (
        P("seq", "tp", "group", None),
        P("seq", ("group", "tp")),
        P(("group", "tp"), None, None, None),
        P(),
    )
    out_specs = P("seq", "tp", "group", None)
    return jax.shard_map(body, mesh=mesh, in_specs=in_specs, out_specs=out_specs, check_vma=False)
```

time: 86.1 us -> 74.5 us (0.87); the launches traced: 84.8 us -> 74.4 us
  Pallas kernels: 81.8 us -> 72.5 us
  local copies, waits for them, and re-layouts: 2.99 us -> 1.83 us
    pallas_call x1, Pallas kernels: 81.8 us -> 72.5 us  [body(): pl.pallas_call(kernel, out_shape=jax.ShapeDtypeStruct((rows, 128), jnp.bf...]
    reshape x1 -> x0, local copies, waits for them, and re-layouts: 2.27 us -> none  [body(): w = key_value_weight.reshape(160, 2048)]
    unnamed x7 -> x1, local copies, waits for them, and re-layouts: 0.72 us -> 1.83 us
where the time goes in v2:
time: 74.5 us; the launch traced here: 74.4 us
  Pallas kernels  72.5 us (97%)
  local copies, waits for them, and re-layouts  1.83 us (2%)
    pallas_call x1, Pallas kernels, body(): pl.pallas_call(kernel, out_shape=jax.ShapeDtypeStruct((rows, 128), jnp.bf...  72.5 us
    unnamed x1, local copies, waits for them, and re-layouts  1.83 us

profile of v2, /device:TPU:1, one launch (start us, length us, event | category | flops | bytes accessed | tf_op | source)
XLA Modules:
  0.0 74.4 jit_solution(2854777386913335347)
XLA Ops:
  0.0 72.5 %compose.1 = bf16[1024,128]{1,0:T(8,128)(2,1)} custom-call(s32[32]{0:T(128)} %order_ref.1, bf16[1024,128]{1,0:T(8,128)(2,1)} %bitcast.8, bf16[160,512]{1,0:T(8,128)(2,1)} %bitcast.9, bf16[2560,128]{1,0:T(8,128)(2,1)} %bitcast.7), custom_call_target="tpu_custom_call" | custom-call | flops 8999999488 | bytes 2000000 | tf_op jit(solution)/shard_map/compose/pallas_call | solution.py:439
  72.5 1.8 %copy.7 = bf16[512,1,2,128]{3,2,1,0:T(2,128)(2,1)} copy(bf16[512,1,2,128]{3,2,1,0:T(2,128)(2,1)} %bitcast.6) | data formatting | bytes 524288

commit v3 on v2

v3 whole, which is shorter than its diff:
```python
import functools

import jax
import jax.numpy as jnp
from jax import lax
from jax.experimental import pallas as pl
from jax.experimental.pallas import tpu as pltpu
from jax.sharding import PartitionSpec as P

MESH = pl.DeviceIdType.MESH
NX, NY, NZ, NG = 4, 8, 8, 4
QT = 128
ROWS = 256
NEG = -1e30
LOG2E = 1.4426950408889634


def kernel(
    order_ref,
    q_hbm,
    aug_hbm,
    w_hbm,
    out_ref,
    q_ref,
    aug_ref,
    w_ref,
    w_wide,
    w_heads,
    augx,
    wx,
    op,
    om,
    ip,
    im,
    own,
    kvs,
    m_ref,
    l_ref,
    acc_ref,
    sc0,
    sc1,
    out_s,
    ax_r,
    wx_r,
    ws_r,
    rp_r,
    rm_r,
    zg_r,
    zq_r,
    yp_r,
    ym_r,
    far_r,
    sb_r,
    loc,
):
    g = lax.axis_index("group")
    seq = lax.axis_index("seq")
    tp = lax.axis_index("tp")
    y, c = lax.div(seq, 2), lax.rem(seq, 2)
    zh, x = lax.div(tp, NX), lax.rem(tp, NX)
    z = zh * NG + g

    def dev(z=z, y=y, c=c, x=x):
        return (lax.rem(z, NG), y * 2 + c, lax.div(z, NG) * NX + x)

    def remote(src, dst, send, recv, to):
        return pltpu.make_async_remote_copy(
            src_ref=src, dst_ref=dst, send_sem=send, recv_sem=recv, device_id=to, device_id_type=MESH
        )

    def wrap(v, n):
        return lax.rem(v + 4 * n, n)

    x_to = [dev(x=wrap(x + d, NX)) for d in (1, 2, 3)]
    z_next, z_prev = dev(z=wrap(z + 1, NZ)), dev(z=wrap(z - 1, NZ))
    g1, g2, g3 = g + 1 - 2 * lax.rem(g, 2), lax.rem(g + 2, NG), 3 - g
    g_to = [dev(z=zh * NG + v) for v in (g1, g2, g3)]
    y_next, y_prev = dev(y=wrap(y + 1, NY)), dev(y=wrap(y - 1, NY))
    sib = dev(c=1 - c)
    far_next = dev(z=zh * NG + g1, y=wrap(y + 1, NY))
    far_prev = dev(z=zh * NG + g1, y=wrap(y - 1, NY))

    barrier = pltpu.get_barrier_semaphore()
    partners = x_to + [z_next, z_prev] + g_to + [y_next, y_prev, sib, far_next, far_prev]
    for to in partners:
        pl.semaphore_signal(barrier, inc=1, device_id=to, device_id_type=MESH)

    loads = [
        pltpu.make_async_copy(w_hbm, w_ref, loc.at[0]),
        pltpu.make_async_copy(aug_hbm, aug_ref, loc.at[1]),
        pltpu.make_async_copy(q_hbm, q_ref, loc.at[2]),
    ]
    for cp in loads:
        cp.start()
    loads[0].wait()
    w_wide[...] = w_ref[...].astype(jnp.float32)
    for j in range(8):
        for half in (0, 1):
            w_heads[j, :, half * QT : (half + 1) * QT] = w_wide[pl.ds(2 * j + half, 160, stride=16), :].astype(
                jnp.bfloat16
            )
    for h in (0, 1):
        wx[h, x] = w_heads[x + NX * h]
    loads[1].wait()
    for i in range(NG):
        augx[i, x] = aug_ref[:, i * QT : (i + 1) * QT]
    pl.semaphore_wait(barrier, len(partners))

    heads = (1 - zh, zh)
    band = pl.ds(pl.multiple_of(80 * c, 16), 80)

    def send_weights(n):
        for i, d in enumerate((1, 2, 3)):
            src = w_heads.at[wrap(x + d, NX) + NX * heads[n], band]
            remote(src, wx.at[heads[n], x, band], out_s.at[0], wx_r.at[n], x_to[i]).start()

    def arrive_weights(n):
        three = wx.at[0, 0:3, band]
        remote(three, three, out_s.at[0], wx_r.at[n], sib).wait_recv()
        for d in (1, 2, 3):
            slot = wx.at[heads[n], wrap(x - d, NX), band]
            remote(slot, slot, out_s.at[1], ws_r.at[n], sib).start()
        remote(three, three, out_s.at[1], ws_r.at[n], sib).wait_recv()

    quarters = [g, wrap(g - 1, NG), wrap(g + 1, NG), wrap(g + 2, NG)]

    def send_states(j):
        slot = augx.at[quarters[j], x]
        for i in range(3):
            remote(slot, slot, out_s.at[2], ax_r.at[j], x_to[i]).start()

    def arrive_states(j):
        three = augx.at[0, 0:3]
        remote(three, three, out_s.at[2], ax_r.at[j], sib).wait_recv()

    send_weights(0)
    send_states(0)
    send_weights(1)
    for j in (1, 2, 3):
        send_states(j)
    arrive_weights(0)

    def share(target):
        states = augx[lax.rem(target, NG)].reshape(NX * 160, QT)
        weights = wx[lax.div(target, NG)].reshape(NX * 160, 2 * QT)
        return lax.dot_general(
            states, weights, (((0,), (0,)), ((), ())), preferred_element_type=jnp.float32
        )

    def send_p(k, half):
        remote(op.at[k - 1, half], ip.at[k - 1, half], out_s.at[3 + k // 4], rp_r.at[k - 1, half], z_next).start()

    def send_m(k, half):
        remote(om.at[k - 1, half], im.at[k - 1, half], out_s.at[5 + k // 4], rm_r.at[k - 1, half], z_prev).start()

    def got_p(k, half):
        slot = ip.at[k - 1, half]
        remote(slot, slot, out_s.at[3 + k // 4], rp_r.at[k - 1, half], z_next).wait_recv()
        return ip[k - 1, half]

    def got_m(k, half):
        slot = im.at[k - 1, half]
        remote(slot, slot, out_s.at[5 + k // 4], rm_r.at[k - 1, half], z_prev).wait_recv()
        return im[k - 1, half]

    def fill(buf, k, part, halves=(0, 1)):
        for half in halves:
            buf[k - 1, half] = part[:, half * QT : (half + 1) * QT]

    arrive_states(0)
    part = share(wrap(z + 4, NZ))
    fill(op, 4, part, (0,))
    fill(om, 4, part, (1,))
    send_p(4, 0)
    send_m(4, 1)
    arrive_weights(1)
    arrive_states(1)
    fill(op, 3, share(wrap(z + 3, NZ)))
    send_p(3, 1)
    arrive_states(2)
    fill(om, 3, share(wrap(z - 3, NZ)))
    send_m(3, 0)
    op[2, 0] += got_p(4, 0)
    send_p(3, 0)
    om[2, 1] += got_m(4, 1)
    send_m(3, 1)
    arrive_states(3)
    fill(op, 2, share(wrap(z + 2, NZ)))
    fill(om, 2, share(wrap(z - 2, NZ)))
    fill(op, 1, share(wrap(z + 1, NZ)))
    fill(om, 1, share(wrap(z - 1, NZ)))
    own[...] = share(z)
    for k in (3, 2):
        for first in (0, 1):
            hp, hm = 1 - first, first
            op[k - 2, hp] += got_p(k, hp)
            send_p(k - 1, hp)
            om[k - 2, hm] += got_m(k, hm)
            send_m(k - 1, hm)

    low = own[:, :QT] + got_m(1, 0)
    high = own[:, QT:] + got_p(1, 1)
    kvs[0, y, g, c] = (low + got_p(1, 0)).astype(jnp.bfloat16)
    kvs[1, y, g, c] = (high + got_m(1, 1)).astype(jnp.bfloat16)

    def quarter_of_own(e, qt):
        slot = kvs.at[:, y, qt, c]
        return remote(slot, slot, out_s.at[7], zg_r.at[e - 1], g_to[e - 1])

    units = (g, g2, g3)
    far = wrap(y + 4, NY)

    def ring_p(d, u):
        slot = kvs.at[:, wrap(y - d, NY), units[u], c]
        return remote(slot, slot, out_s.at[8], yp_r.at[d, u], y_next)

    def ring_m(d, u):
        slot = kvs.at[:, wrap(y + d, NY), units[u], c]
        return remote(slot, slot, out_s.at[9], ym_r.at[d, u], y_prev)

    def arrive_p(d, u):
        slot = kvs.at[:, wrap(y - d, NY), units[u], c]
        remote(slot, slot, out_s.at[8], yp_r.at[d - 1, u], y_next).wait_recv()

    def arrive_m(d, u):
        slot = kvs.at[:, wrap(y + d, NY), units[u], c]
        remote(slot, slot, out_s.at[9], ym_r.at[d - 1, u], y_prev).wait_recv()

    def swap(yi, d):
        slot = kvs.at[:, yi, g, c]
        remote(slot, slot, out_s.at[10], zq_r.at[d - 1], g_to[0]).start()

    def far_p(qt):
        slot = kvs.at[:, wrap(y - 3, NY), qt, c]
        return remote(slot, slot, out_s.at[11], far_r.at[0], far_next)

    def far_m(qt):
        slot = kvs.at[:, wrap(y + 3, NY), qt, c]
        return remote(slot, slot, out_s.at[11], far_r.at[1], far_prev)

    def share_core(group, yi, qt):
        slot = kvs.at[:, yi, qt, c]
        remote(slot, slot, out_s.at[12], sb_r.at[group], sib).start()

    def from_sibling(group):
        four = kvs.at[:, 0:2, 0:2, 0]
        remote(four, four, out_s.at[12], sb_r.at[group], sib).wait_recv()

    def own_unit(u):
        quarter_of_own(u + 1, units[u]).wait_recv()
        ring_p(0, u).start()
        ring_m(0, u).start()
        share_core(0, y, units[u])

    ring_p(0, 0).start()
    ring_m(0, 0).start()
    for e in (2, 3, 1):
        quarter_of_own(e, g).start()
    share_core(0, y, g)
    loads[2].wait()

    scale = LOG2E * 128 ** -0.5
    scores = (sc0, sc1)

    def score(pairs, rb, s):
        q = q_ref[rb * ROWS : (rb + 1) * ROWS, :]
        for h, (yi, qt) in enumerate(pairs):
            keys = kvs[0, yi, qt].reshape(2 * QT, QT)
            s[:, h * 256 : (h + 1) * 256] = lax.dot_general(
                q, keys, (((1,), (1,)), ((), ())), preferred_element_type=jnp.float32
            )

    def weigh(pairs, rb, s, diagonal):
        rows = slice(rb * ROWS, (rb + 1) * ROWS)
        n = len(pairs)
        qo = order_ref[2 * seq + rb * ROWS // 512]
        parts = [s[:, i * QT : (i + 1) * QT] for i in range(2 * n)]
        places = [order_ref[4 * yi + 2 * ci + lax.div(qt, 2)] for yi, qt in pairs for ci in (0, 1)]
        if diagonal:
            row = lax.broadcasted_iota(jnp.int32, (ROWS, QT), 0) + (rb * ROWS) % 512
            ahead = lax.shift_right_logical(row, 1) - lax.broadcasted_iota(jnp.int32, (ROWS, QT), 1)
            for i in range(2 * n):
                start = (places[i] - qo) * 256 + lax.rem(pairs[i // 2][1], 2) * QT
                parts[i] = jnp.where(ahead >= start, parts[i], NEG)
            tops = parts
        else:
            bias = [jnp.where(place < qo, 0.0, NEG) for place in places]
            tops = [parts[i] + bias[i] for i in range(2 * n)]
        top = functools.reduce(jnp.maximum, tops)
        new = jnp.broadcast_to(jnp.max(top, axis=-1, keepdims=True), (ROWS, QT))
        if not diagonal:
            old = m_ref[rows, :]
            new = jnp.maximum(old, new)
        m_ref[rows, :] = new
        total, o = None, None
        for h, (yi, qt) in enumerate(pairs):
            pair = []
            for i in (2 * h, 2 * h + 1):
                base = new if diagonal else new - bias[i]
                pair.append(jnp.exp2((parts[i] - base) * scale))
            t = pair[0] + pair[1]
            total = t if total is None else total + t
            probs = jnp.concatenate([v.astype(jnp.bfloat16) for v in pair], axis=1)
            values = kvs[1, yi, qt].reshape(2 * QT, QT)
            t = jnp.dot(probs, values, preferred_element_type=jnp.float32)
            o = t if o is None else o + t
        if diagonal:
            l_ref[rows, :] = total
            acc_ref[rows, :] = o
        else:
            alpha = jnp.exp2((old - new) * scale)
            l_ref[rows, :] = l_ref[rows, :] * alpha + total
            acc_ref[rows, :] = acc_ref[rows, :] * alpha + o

    def pairs_of(d, first):
        behind, before = wrap(y - d, NY), wrap(y + d, NY)
        return [(yi, qt) for qt in ((g, g2) if first else (g3, g1)) for yi in (behind, before)]

    chunks = [[(y, qt) for qt in range(NG)]]
    for d in (1, 2, 3):
        chunks += [pairs_of(d, True), pairs_of(d, False)]
    chunks.append([(far, qt) for qt in (g, g1, g2, g3)])
    state = {"next": 0, "scored": 0, "ready": 0}

    def ready(group):
        from_sibling(group)
        state["ready"] += 4

    def work(count):
        for _ in range(count):
            k = state["next"]
            while state["scored"] < min(k + 2, state["ready"]):
                n = state["scored"]
                score(chunks[n // 4], n % 4, scores[n % 2])
                state["scored"] += 1
            weigh(chunks[k // 4], k % 4, scores[k % 2], k < 4)
            state["next"] += 1

    def unit(d, u):
        new_p, new_m = wrap(y - d, NY), wrap(y + d, NY)
        group = 2 * d - (1 if u < 2 else 0)
        arrive_p(d, u)
        if d < 3 or u == 0:
            ring_p(d, u).start()
        if u == 0:
            if d == 3:
                far_p(g).start()
            swap(new_p, d)
        share_core(group, new_p, units[u])
        arrive_m(d, u)
        if d < 3 or u == 1:
            ring_m(d, u).start()
        if u == 1 and d == 3:
            far_m(g2).start()
        if u == 0:
            swap(new_m, d)
        share_core(group, new_m, units[u])

    def swapped(d):
        two = kvs.at[:, y, 0:2, c]
        remote(two, two, out_s.at[10], zq_r.at[d - 1], sib).wait_recv()
        share_core(2 * d, wrap(y - d, NY), g1)
        share_core(2 * d, wrap(y + d, NY), g1)

    own_unit(1)
    unit(1, 0)
    own_unit(2)
    quarter_of_own(1, g1).wait_recv()
    share_core(0, y, g1)
    ready(0)
    work(2)
    unit(2, 0)
    unit(1, 1)
    work(1)
    swapped(1)
    unit(1, 2)
    work(1)
    ready(1)
    work(2)
    unit(3, 0)
    work(1)
    unit(2, 1)
    swapped(2)
    ready(2)
    work(2)
    unit(2, 2)
    work(3)
    arrive_p(4, 0)
    share_core(7, far, g)
    ready(3)
    work(1)
    unit(3, 1)
    swapped(3)
    work(2)
    unit(3, 2)
    ready(4)
    work(4)
    arrive_m(4, 1)
    share_core(7, far, g2)
    ready(5)
    work(4)
    for i, qt in ((0, g1), (1, g3)):
        slot = kvs.at[:, far, qt, c]
        remote(slot, slot, out_s.at[11], far_r.at[i], sib).wait_recv()
        share_core(7, far, qt)
    ready(6)
    work(3)
    ready(7)
    work(len(chunks) * 4 - state["next"])

    out_ref[...] = (acc_ref[...] / jnp.sum(l_ref[...], axis=-1, keepdims=True)).astype(jnp.bfloat16)

    sent = [
        w_heads.at[0:3],
        w_heads.at[0:3],
        augx.at[0:3],
        op.at[0:3],
        op.at[3, 0],
        om.at[0:3],
        om.at[3, 1],
        kvs.at[:, 0, 0:3, 0],
        kvs.at[:, 0:5, 0:2, 0],
        kvs.at[:, 0:5, 0:2, 0],
        kvs.at[:, 0:3, 0:2, 0],
        kvs.at[:, 0, 0:2, 0],
        kvs.at[:, :, :, 0],
    ]
    for i, ref in enumerate(sent):
        remote(ref, ref, out_s.at[i], far_r.at[0], sib).wait_send()


def body(queries, aug_states, key_value_weight, block_order):
    tok = queries.shape[0]
    rows = tok * queries.shape[2]
    q = queries.reshape(rows, 128)
    aug = aug_states.T
    w = key_value_weight.reshape(2560, 128)
    dma = pltpu.SemaphoreType.DMA
    out = pl.pallas_call(
        kernel,
        out_shape=jax.ShapeDtypeStruct((rows, 128), jnp.bfloat16),
        in_specs=[pl.BlockSpec(memory_space=pltpu.SMEM)] + [pl.BlockSpec(memory_space=pltpu.HBM)] * 3,
        out_specs=pl.BlockSpec(memory_space=pltpu.VMEM),
        scratch_shapes=[
            pltpu.VMEM((rows, 128), jnp.bfloat16),
            pltpu.VMEM((160, 512), jnp.bfloat16),
            pltpu.VMEM((2560, 128), jnp.bfloat16),
            pltpu.VMEM((2560, 128), jnp.float32),
            pltpu.VMEM((8, 160, 2 * QT), jnp.bfloat16),
            pltpu.VMEM((NG, NX, 160, QT), jnp.bfloat16),
            pltpu.VMEM((2, NX, 160, 2 * QT), jnp.bfloat16),
            pltpu.VMEM((4, 2, QT, QT), jnp.float32),
            pltpu.VMEM((4, 2, QT, QT), jnp.float32),
            pltpu.VMEM((4, 2, QT, QT), jnp.float32),
            pltpu.VMEM((4, 2, QT, QT), jnp.float32),
            pltpu.VMEM((QT, 2 * QT), jnp.float32),
            pltpu.VMEM((2, NY, NG, 2, QT, QT), jnp.bfloat16),
            pltpu.VMEM((rows, 128), jnp.float32),
            pltpu.VMEM((rows, 128), jnp.float32),
            pltpu.VMEM((rows, 128), jnp.float32),
            pltpu.VMEM((ROWS, 8 * QT), jnp.float32),
            pltpu.VMEM((ROWS, 8 * QT), jnp.float32),
            dma((13,)),
            dma((4,)),
            dma((2,)),
            dma((2,)),
            dma((4, 2)),
            dma((4, 2)),
            dma((3,)),
            dma((3,)),
            dma((4, 3)),
            dma((4, 3)),
            dma((2,)),
            dma((8,)),
            dma((3,)),
        ],
        compiler_params=pltpu.CompilerParams(
            collective_id=0, has_side_effects=True, vmem_limit_bytes=62 * 1024 * 1024
        ),
        cost_estimate=pl.CostEstimate(flops=9 * 10**9, bytes_accessed=2 * 10**6, transcendentals=8 * 10**6),
        name="compose",
    )(block_order, q, aug, w)
    return out.reshape(queries.shape)


def solution(mesh):
    in_specs = (
        P("seq", "tp", "group", None),
        P("seq", ("group", "tp")),
        P(("group", "tp"), None, None, None),
        P(),
    )
    out_specs = P("seq", "tp", "group", None)
    return jax.shard_map(body, mesh=mesh, in_specs=in_specs, out_specs=out_specs, check_vma=False)
```

time: 74.5 us -> 72.1 us (0.968)
  Pallas kernels: 72.5 us -> 70.1 us
    pallas_call x1, Pallas kernels: 72.5 us -> 70.1 us  [body(): pl.pallas_call(kernel, out_shape=jax.ShapeDtypeStruct((rows, 128), jnp.bf...]
where the time goes in v3:
time: 72.1 us; the launch traced here: 71.9 us
  Pallas kernels  70.1 us (97%)
  local copies, waits for them, and re-layouts  1.83 us (3%)
    pallas_call x1, Pallas kernels, body(): pl.pallas_call(kernel, out_shape=jax.ShapeDtypeStruct((rows, 128), jnp.bf...  70.1 us
    unnamed x1, local copies, waits for them, and re-layouts  1.83 us

profile of v3, /device:TPU:1, one launch (start us, length us, event | category | flops | bytes accessed | tf_op | source)
XLA Modules:
  0.0 71.9 jit_solution(14509454557535412100)
XLA Ops:
  0.0 70.1 %compose.1 = bf16[1024,128]{1,0:T(8,128)(2,1)} custom-call(s32[32]{0:T(128)} %order_ref.1, bf16[1024,128]{1,0:T(8,128)(2,1)} %bitcast.8, bf16[160,512]{1,0:T(8,128)(2,1)} %bitcast.9, bf16[2560,128]{1,0:T(8,128)(2,1)} %bitcast.7), custom_call_target="tpu_custom_call" | custom-call | flops 8999999488 | bytes 2000000 | tf_op jit(solution)/shard_map/compose/pallas_call | solution.py:439
  70.1 1.8 %copy.7 = bf16[512,1,2,128]{3,2,1,0:T(2,128)(2,1)} copy(bf16[512,1,2,128]{3,2,1,0:T(2,128)(2,1)} %bitcast.6) | data formatting | bytes 524288

commit v4 on v3

--- a/solution.py
+++ b/solution.py
@@ -10,6 +10,7 @@
 MESH = pl.DeviceIdType.MESH
 NX, NY, NZ, NG = 4, 8, 8, 4
 QT = 128
+HALF = 64
 ROWS = 256
 NEG = -1e30
 LOG2E = 1.4426950408889634
@@ -147,43 +148,50 @@
             states, weights, (((0,), (0,)), ((), ())), preferred_element_type=jnp.float32
         )
 
-    def send_p(k, half):
-        remote(op.at[k - 1, half], ip.at[k - 1, half], out_s.at[3 + k // 4], rp_r.at[k - 1, half], z_next).start()
-
-    def send_m(k, half):
-        remote(om.at[k - 1, half], im.at[k - 1, half], out_s.at[5 + k // 4], rm_r.at[k - 1, half], z_prev).start()
-
-    def got_p(k, half):
-        slot = ip.at[k - 1, half]
-        remote(slot, slot, out_s.at[3 + k // 4], rp_r.at[k - 1, half], z_next).wait_recv()
-        return ip[k - 1, half]
-
-    def got_m(k, half):
-        slot = im.at[k - 1, half]
-        remote(slot, slot, out_s.at[5 + k // 4], rm_r.at[k - 1, half], z_prev).wait_recv()
-        return im[k - 1, half]
+    def send_p(k, kind, r):
+        at = (k - 1, kind, r)
+        remote(op.at[at], ip.at[at], out_s.at[3 + k // 4], rp_r.at[at], z_next).start()
+
+    def send_m(k, kind, r):
+        at = (k - 1, kind, r)
+        remote(om.at[at], im.at[at], out_s.at[5 + k // 4], rm_r.at[at], z_prev).start()
+
+    def got_p(k, kind, r):
+        at = (k - 1, kind, r)
+        remote(ip.at[at], ip.at[at], out_s.at[3 + k // 4], rp_r.at[at], z_next).wait_recv()
+        return ip[at]
+
+    def got_m(k, kind, r):
+        at = (k - 1, kind, r)
+        remote(im.at[at], im.at[at], out_s.at[5 + k // 4], rm_r.at[at], z_prev).wait_recv()
+        return im[at]
 
     def fill(buf, k, part, halves=(0, 1)):
-        for half in halves:
-            buf[k - 1, half] = part[:, half * QT : (half + 1) * QT]
+        for kind in (0, 1):
+            for r in halves:
+                buf[k - 1, kind, r] = part[r * HALF : (r + 1) * HALF, kind * QT : (kind + 1) * QT]
 
     arrive_states(0)
     part = share(wrap(z + 4, NZ))
     fill(op, 4, part, (0,))
     fill(om, 4, part, (1,))
-    send_p(4, 0)
-    send_m(4, 1)
+    for kind in (0, 1):
+        send_p(4, kind, 0)
+        send_m(4, kind, 1)
     arrive_weights(1)
     arrive_states(1)
     fill(op, 3, share(wrap(z + 3, NZ)))
-    send_p(3, 1)
+    for kind in (0, 1):
+        send_p(3, kind, 1)
     arrive_states(2)
     fill(om, 3, share(wrap(z - 3, NZ)))
-    send_m(3, 0)
-    op[2, 0] += got_p(4, 0)
-    send_p(3, 0)
-    om[2, 1] += got_m(4, 1)
-    send_m(3, 1)
+    for kind in (0, 1):
+        send_m(3, kind, 0)
+    for kind in (0, 1):
+        op[2, kind, 0] += got_p(4, kind, 0)
+        send_p(3, kind, 0)
+        om[2, kind, 1] += got_m(4, kind, 1)
+        send_m(3, kind, 1)
     arrive_states(3)
     fill(op, 2, share(wrap(z + 2, NZ)))
     fill(om, 2, share(wrap(z - 2, NZ)))
@@ -191,59 +199,61 @@
     fill(om, 1, share(wrap(z - 1, NZ)))
     own[...] = share(z)
     for k in (3, 2):
-        for first in (0, 1):
-            hp, hm = 1 - first, first
-            op[k - 2, hp] += got_p(k, hp)
-            send_p(k - 1, hp)
-            om[k - 2, hm] += got_m(k, hm)
-            send_m(k - 1, hm)
-
-    low = own[:, :QT] + got_m(1, 0)
-    high = own[:, QT:] + got_p(1, 1)
-    kvs[0, y, g, c] = (low + got_p(1, 0)).astype(jnp.bfloat16)
-    kvs[1, y, g, c] = (high + got_m(1, 1)).astype(jnp.bfloat16)
+        for kind in (0, 1):
+            for first in (0, 1):
+                rp, rm = 1 - first, first
+                op[k - 2, kind, rp] += got_p(k, kind, rp)
+                send_p(k - 1, kind, rp)
+                om[k - 2, kind, rm] += got_m(k, kind, rm)
+                send_m(k - 1, kind, rm)
+
+    def finish(kind):
+        for r in (0, 1):
+            rows = slice(r * HALF, (r + 1) * HALF)
+            total = own[rows, kind * QT : (kind + 1) * QT] + got_m(1, kind, r) + got_p(1, kind, r)
+            kvs[y, g, c, kind, rows] = total.astype(jnp.bfloat16)
 
     def quarter_of_own(e, qt):
-        slot = kvs.at[:, y, qt, c]
+        slot = kvs.at[y, qt, c]
         return remote(slot, slot, out_s.at[7], zg_r.at[e - 1], g_to[e - 1])
 
     units = (g, g2, g3)
     far = wrap(y + 4, NY)
 
     def ring_p(d, u):
-        slot = kvs.at[:, wrap(y - d, NY), units[u], c]
+        slot = kvs.at[wrap(y - d, NY), units[u], c]
         return remote(slot, slot, out_s.at[8], yp_r.at[d, u], y_next)
 
     def ring_m(d, u):
-        slot = kvs.at[:, wrap(y + d, NY), units[u], c]
+        slot = kvs.at[wrap(y + d, NY), units[u], c]
         return remote(slot, slot, out_s.at[9], ym_r.at[d, u], y_prev)
 
     def arrive_p(d, u):
-        slot = kvs.at[:, wrap(y - d, NY), units[u], c]
+        slot = kvs.at[wrap(y - d, NY), units[u], c]
         remote(slot, slot, out_s.at[8], yp_r.at[d - 1, u], y_next).wait_recv()
 
     def arrive_m(d, u):
-        slot = kvs.at[:, wrap(y + d, NY), units[u], c]
+        slot = kvs.at[wrap(y + d, NY), units[u], c]
         remote(slot, slot, out_s.at[9], ym_r.at[d - 1, u], y_prev).wait_recv()
 
     def swap(yi, d):
-        slot = kvs.at[:, yi, g, c]
+        slot = kvs.at[yi, g, c]
         remote(slot, slot, out_s.at[10], zq_r.at[d - 1], g_to[0]).start()
 
     def far_p(qt):
-        slot = kvs.at[:, wrap(y - 3, NY), qt, c]
+        slot = kvs.at[wrap(y - 3, NY), qt, c]
         return remote(slot, slot, out_s.at[11], far_r.at[0], far_next)
 
     def far_m(qt):
-        slot = kvs.at[:, wrap(y + 3, NY), qt, c]
+        slot = kvs.at[wrap(y + 3, NY), qt, c]
         return remote(slot, slot, out_s.at[11], far_r.at[1], far_prev)
 
     def share_core(group, yi, qt):
-        slot = kvs.at[:, yi, qt, c]
+        slot = kvs.at[yi, qt, c]
         remote(slot, slot, out_s.at[12], sb_r.at[group], sib).start()
 
     def from_sibling(group):
-        four = kvs.at[:, 0:2, 0:2, 0]
+        four = kvs.at[0, :, 0]
         remote(four, four, out_s.at[12], sb_r.at[group], sib).wait_recv()
 
     def own_unit(u):
@@ -252,10 +262,13 @@
         ring_m(0, u).start()
         share_core(0, y, units[u])
 
-    ring_p(0, 0).start()
-    ring_m(0, 0).start()
-    for e in (2, 3, 1):
-        quarter_of_own(e, g).start()
+    for kind in (0, 1):
+        finish(kind)
+        slot = kvs.at[y, g, c, kind]
+        remote(slot, slot, out_s.at[8], yp_r.at[0, 0], y_next).start()
+        remote(slot, slot, out_s.at[9], ym_r.at[0, 0], y_prev).start()
+        for e in (2, 3, 1):
+            remote(slot, slot, out_s.at[7], zg_r.at[e - 1], g_to[e - 1]).start()
     share_core(0, y, g)
     loads[2].wait()
 
@@ -265,7 +278,7 @@
     def score(pairs, rb, s):
         q = q_ref[rb * ROWS : (rb + 1) * ROWS, :]
         for h, (yi, qt) in enumerate(pairs):
-            keys = kvs[0, yi, qt].reshape(2 * QT, QT)
+            keys = jnp.concatenate([kvs[yi, qt, 0, 0], kvs[yi, qt, 1, 0]], axis=0)
             s[:, h * 256 : (h + 1) * 256] = lax.dot_general(
                 q, keys, (((1,), (1,)), ((), ())), preferred_element_type=jnp.float32
             )
@@ -301,7 +314,7 @@
             t = pair[0] + pair[1]
             total = t if total is None else total + t
             probs = jnp.concatenate([v.astype(jnp.bfloat16) for v in pair], axis=1)
-            values = kvs[1, yi, qt].reshape(2 * QT, QT)
+            values = jnp.concatenate([kvs[yi, qt, 0, 1], kvs[yi, qt, 1, 1]], axis=0)
             t = jnp.dot(probs, values, preferred_element_type=jnp.float32)
             o = t if o is None else o + t
         if diagonal:
@@ -357,7 +370,7 @@
         share_core(group, new_m, units[u])
 
     def swapped(d):
-        two = kvs.at[:, y, 0:2, c]
+        two = kvs.at[y, 0:2, c]
         remote(two, two, out_s.at[10], zq_r.at[d - 1], sib).wait_recv()
         share_core(2 * d, wrap(y - d, NY), g1)
         share_core(2 * d, wrap(y + d, NY), g1)
@@ -400,7 +413,7 @@
     ready(5)
     work(4)
     for i, qt in ((0, g1), (1, g3)):
-        slot = kvs.at[:, far, qt, c]
+        slot = kvs.at[far, qt, c]
         remote(slot, slot, out_s.at[11], far_r.at[i], sib).wait_recv()
         share_core(7, far, qt)
     ready(6)
@@ -415,15 +428,15 @@
         w_heads.at[0:3],
         augx.at[0:3],
         op.at[0:3],
-        op.at[3, 0],
+        op.at[3, :, 0],
         om.at[0:3],
-        om.at[3, 1],
-        kvs.at[:, 0, 0:3, 0],
-        kvs.at[:, 0:5, 0:2, 0],
-        kvs.at[:, 0:5, 0:2, 0],
-        kvs.at[:, 0:3, 0:2, 0],
-        kvs.at[:, 0, 0:2, 0],
-        kvs.at[:, :, :, 0],
+        om.at[3, :, 1],
+        kvs.at[0, 0:3, 0],
+        kvs.at[0:5, 0:2, 0],
+        kvs.at[0:5, 0:2, 0],
+        kvs.at[0:3, 0:2, 0],
+        kvs.at[0, 0:2, 0],
+        kvs.at[:, :, 0],
     ]
     for i, ref in enumerate(sent):
         remote(ref, ref, out_s.at[i], far_r.at[0], sib).wait_send()
@@ -449,12 +462,12 @@
             pltpu.VMEM((8, 160, 2 * QT), jnp.bfloat16),
             pltpu.VMEM((NG, NX, 160, QT), jnp.bfloat16),
             pltpu.VMEM((2, NX, 160, 2 * QT), jnp.bfloat16),
-            pltpu.VMEM((4, 2, QT, QT), jnp.float32),
-            pltpu.VMEM((4, 2, QT, QT), jnp.float32),
-            pltpu.VMEM((4, 2, QT, QT), jnp.float32),
-            pltpu.VMEM((4, 2, QT, QT), jnp.float32),
+            pltpu.VMEM((4, 2, 2, HALF, QT), jnp.float32),
+            pltpu.VMEM((4, 2, 2, HALF, QT), jnp.float32),
+            pltpu.VMEM((4, 2, 2, HALF, QT), jnp.float32),
+            pltpu.VMEM((4, 2, 2, HALF, QT), jnp.float32),
             pltpu.VMEM((QT, 2 * QT), jnp.float32),
-            pltpu.VMEM((2, NY, NG, 2, QT, QT), jnp.bfloat16),
+            pltpu.VMEM((NY, NG, 2, 2, QT, QT), jnp.bfloat16),
             pltpu.VMEM((rows, 128), jnp.float32),
             pltpu.VMEM((rows, 128), jnp.float32),
             pltpu.VMEM((rows, 128), jnp.float32),
@@ -464,8 +477,8 @@
             dma((4,)),
             dma((2,)),
             dma((2,)),
-            dma((4, 2)),
-            dma((4, 2)),
+            dma((4, 2, 2)),
+            dma((4, 2, 2)),
             dma((3,)),
             dma((3,)),
             dma((4, 3)),

time: 72.1 us -> 70.6 us (0.979)
  Pallas kernels: 70.1 us -> 68.6 us
    pallas_call x1, Pallas kernels: 70.1 us -> 68.6 us  [body(): pl.pallas_call(kernel, out_shape=jax.ShapeDtypeStruct((rows, 128), jnp.bf...]
where the time goes in v4:
time: 70.6 us; the launch traced here: 70.4 us
  Pallas kernels  68.6 us (97%)
  local copies, waits for them, and re-layouts  1.83 us (3%)
    pallas_call x1, Pallas kernels, body(): pl.pallas_call(kernel, out_shape=jax.ShapeDtypeStruct((rows, 128), jnp.bf...  68.6 us
    unnamed x1, local copies, waits for them, and re-layouts  1.83 us

profile of v4, /device:TPU:1, one launch (start us, length us, event | category | flops | bytes accessed | tf_op | source)
XLA Modules:
  0.0 70.4 jit_solution(6830676690480758202)
XLA Ops:
  0.0 68.6 %compose.1 = bf16[1024,128]{1,0:T(8,128)(2,1)} custom-call(s32[32]{0:T(128)} %order_ref.1, bf16[1024,128]{1,0:T(8,128)(2,1)} %bitcast.8, bf16[160,512]{1,0:T(8,128)(2,1)} %bitcast.9, bf16[2560,128]{1,0:T(8,128)(2,1)} %bitcast.7), custom_call_target="tpu_custom_call" | custom-call | flops 8999999488 | bytes 2000000 | tf_op jit(solution)/shard_map/compose/pallas_call | solution.py:452
  68.6 1.8 %copy.7 = bf16[512,1,2,128]{3,2,1,0:T(2,128)(2,1)} copy(bf16[512,1,2,128]{3,2,1,0:T(2,128)(2,1)} %bitcast.6) | data formatting | bytes 524288

commit v5 on v4

--- a/solution.py
+++ b/solution.py
@@ -78,11 +78,10 @@
     g_to = [dev(z=zh * NG + v) for v in (g1, g2, g3)]
     y_next, y_prev = dev(y=wrap(y + 1, NY)), dev(y=wrap(y - 1, NY))
     sib = dev(c=1 - c)
-    far_next = dev(z=zh * NG + g1, y=wrap(y + 1, NY))
-    far_prev = dev(z=zh * NG + g1, y=wrap(y - 1, NY))
+    across = dev(y=wrap(y + 4, NY))
 
     barrier = pltpu.get_barrier_semaphore()
-    partners = x_to + [z_next, z_prev] + g_to + [y_next, y_prev, sib, far_next, far_prev]
+    partners = x_to + [z_next, z_prev] + g_to + [y_next, y_prev, sib, across]
     for to in partners:
         pl.semaphore_signal(barrier, inc=1, device_id=to, device_id_type=MESH)
 
@@ -240,13 +239,13 @@
         slot = kvs.at[yi, g, c]
         remote(slot, slot, out_s.at[10], zq_r.at[d - 1], g_to[0]).start()
 
-    def far_p(qt):
-        slot = kvs.at[wrap(y - 3, NY), qt, c]
-        return remote(slot, slot, out_s.at[11], far_r.at[0], far_next)
-
-    def far_m(qt):
-        slot = kvs.at[wrap(y + 3, NY), qt, c]
-        return remote(slot, slot, out_s.at[11], far_r.at[1], far_prev)
+    def far_own():
+        slot = kvs.at[far, g, c]
+        return remote(slot, slot, out_s.at[11], far_r.at[0], across)
+
+    def far_quarter(e, qt):
+        slot = kvs.at[far, qt, c]
+        return remote(slot, slot, out_s.at[7], far_r.at[e], g_to[e - 1])
 
     def share_core(group, yi, qt):
         slot = kvs.at[yi, qt, c]
@@ -269,37 +268,36 @@
         remote(slot, slot, out_s.at[9], ym_r.at[0, 0], y_prev).start()
         for e in (2, 3, 1):
             remote(slot, slot, out_s.at[7], zg_r.at[e - 1], g_to[e - 1]).start()
+    mine = kvs.at[y, g, c]
+    remote(mine, mine, out_s.at[11], far_r.at[0], across).start()
     share_core(0, y, g)
     loads[2].wait()
 
     scale = LOG2E * 128 ** -0.5
     scores = (sc0, sc1)
 
-    def score(pairs, rb, s):
+    def score(pairs, rb, s, diagonal):
         q = q_ref[rb * ROWS : (rb + 1) * ROWS, :]
-        for h, (yi, qt) in enumerate(pairs):
-            keys = jnp.concatenate([kvs[yi, qt, 0, 0], kvs[yi, qt, 1, 0]], axis=0)
-            s[:, h * 256 : (h + 1) * 256] = lax.dot_general(
-                q, keys, (((1,), (1,)), ((), ())), preferred_element_type=jnp.float32
-            )
-
-    def weigh(pairs, rb, s, diagonal):
-        rows = slice(rb * ROWS, (rb + 1) * ROWS)
-        n = len(pairs)
         qo = order_ref[2 * seq + rb * ROWS // 512]
-        parts = [s[:, i * QT : (i + 1) * QT] for i in range(2 * n)]
-        places = [order_ref[4 * yi + 2 * ci + lax.div(qt, 2)] for yi, qt in pairs for ci in (0, 1)]
         if diagonal:
             row = lax.broadcasted_iota(jnp.int32, (ROWS, QT), 0) + (rb * ROWS) % 512
             ahead = lax.shift_right_logical(row, 1) - lax.broadcasted_iota(jnp.int32, (ROWS, QT), 1)
-            for i in range(2 * n):
-                start = (places[i] - qo) * 256 + lax.rem(pairs[i // 2][1], 2) * QT
-                parts[i] = jnp.where(ahead >= start, parts[i], NEG)
-            tops = parts
-        else:
-            bias = [jnp.where(place < qo, 0.0, NEG) for place in places]
-            tops = [parts[i] + bias[i] for i in range(2 * n)]
-        top = functools.reduce(jnp.maximum, tops)
+        for h, (yi, qt) in enumerate(pairs):
+            keys = jnp.concatenate([kvs[yi, qt, 0, 0], kvs[yi, qt, 1, 0]], axis=0)
+            both = lax.dot_general(q, keys, (((1,), (1,)), ((), ())), preferred_element_type=jnp.float32) * scale
+            for ci in (0, 1):
+                place = order_ref[4 * yi + 2 * ci + lax.div(qt, 2)]
+                part = both[:, ci * QT : (ci + 1) * QT]
+                if diagonal:
+                    part = jnp.where(ahead >= (place - qo) * 256 + lax.rem(qt, 2) * QT, part, NEG)
+                else:
+                    part = part + jnp.where(place < qo, 0.0, NEG)
+                s[:, (2 * h + ci) * QT : (2 * h + ci + 1) * QT] = part
+
+    def weigh(pairs, rb, s, diagonal):
+        rows = slice(rb * ROWS, (rb + 1) * ROWS)
+        parts = [s[:, i * QT : (i + 1) * QT] for i in range(2 * len(pairs))]
+        top = functools.reduce(jnp.maximum, parts)
         new = jnp.broadcast_to(jnp.max(top, axis=-1, keepdims=True), (ROWS, QT))
         if not diagonal:
             old = m_ref[rows, :]
@@ -307,10 +305,7 @@
         m_ref[rows, :] = new
         total, o = None, None
         for h, (yi, qt) in enumerate(pairs):
-            pair = []
-            for i in (2 * h, 2 * h + 1):
-                base = new if diagonal else new - bias[i]
-                pair.append(jnp.exp2((parts[i] - base) * scale))
+            pair = [jnp.exp2(parts[2 * h + ci] - new) for ci in (0, 1)]
             t = pair[0] + pair[1]
             total = t if total is None else total + t
             probs = jnp.concatenate([v.astype(jnp.bfloat16) for v in pair], axis=1)
@@ -321,7 +316,7 @@
             l_ref[rows, :] = total
             acc_ref[rows, :] = o
         else:
-            alpha = jnp.exp2((old - new) * scale)
+            alpha = jnp.exp2(old - new)
             l_ref[rows, :] = l_ref[rows, :] * alpha + total
             acc_ref[rows, :] = acc_ref[rows, :] * alpha + o
 
@@ -332,7 +327,7 @@
     chunks = [[(y, qt) for qt in range(NG)]]
     for d in (1, 2, 3):
         chunks += [pairs_of(d, True), pairs_of(d, False)]
-    chunks.append([(far, qt) for qt in (g, g1, g2, g3)])
+    chunks.insert(4, [(far, qt) for qt in (g, g1, g2, g3)])
     state = {"next": 0, "scored": 0, "ready": 0}
 
     def ready(group):
@@ -344,7 +339,7 @@
             k = state["next"]
             while state["scored"] < min(k + 2, state["ready"]):
                 n = state["scored"]
-                score(chunks[n // 4], n % 4, scores[n % 2])
+                score(chunks[n // 4], n % 4, scores[n % 2], n < 4)
                 state["scored"] += 1
             weigh(chunks[k // 4], k % 4, scores[k % 2], k < 4)
             state["next"] += 1
@@ -353,18 +348,14 @@
         new_p, new_m = wrap(y - d, NY), wrap(y + d, NY)
         group = 2 * d - (1 if u < 2 else 0)
         arrive_p(d, u)
-        if d < 3 or u == 0:
+        if d < 3:
             ring_p(d, u).start()
         if u == 0:
-            if d == 3:
-                far_p(g).start()
             swap(new_p, d)
         share_core(group, new_p, units[u])
         arrive_m(d, u)
-        if d < 3 or u == 1:
+        if d < 3:
             ring_m(d, u).start()
-        if u == 1 and d == 3:
-            far_m(g2).start()
         if u == 0:
             swap(new_m, d)
         share_core(group, new_m, units[u])
@@ -380,6 +371,10 @@
     own_unit(2)
     quarter_of_own(1, g1).wait_recv()
     share_core(0, y, g1)
+    far_own().wait_recv()
+    for e in (2, 3, 1):
+        far_quarter(e, g).start()
+    share_core(7, far, g)
     ready(0)
     work(2)
     unit(2, 0)
@@ -398,28 +393,21 @@
     work(2)
     unit(2, 2)
     work(3)
-    arrive_p(4, 0)
-    share_core(7, far, g)
     ready(3)
     work(1)
+    for e, qt in ((1, g1), (2, g2), (3, g3)):
+        far_quarter(e, qt).wait_recv()
+        share_core(7, far, qt)
     unit(3, 1)
     swapped(3)
+    work(3)
+    ready(7)
     work(2)
     unit(3, 2)
-    ready(4)
-    work(4)
-    arrive_m(4, 1)
-    share_core(7, far, g2)
-    ready(5)
-    work(4)
-    for i, qt in ((0, g1), (1, g3)):
-        slot = kvs.at[far, qt, c]
-        remote(slot, slot, out_s.at[11], far_r.at[i], sib).wait_recv()
-        share_core(7, far, qt)
-    ready(6)
-    work(3)
-    ready(7)
-    work(len(chunks) * 4 - state["next"])
+    work(2)
+    for group in (4, 5, 6):
+        ready(group)
+        work(4)
 
     out_ref[...] = (acc_ref[...] / jnp.sum(l_ref[...], axis=-1, keepdims=True)).astype(jnp.bfloat16)
 
@@ -431,11 +419,11 @@
         op.at[3, :, 0],
         om.at[0:3],
         om.at[3, :, 1],
-        kvs.at[0, 0:3, 0],
-        kvs.at[0:5, 0:2, 0],
-        kvs.at[0:5, 0:2, 0],
+        kvs.at[0:2, 0:3, 0],
+        kvs.at[0:3, 0:3, 0],
+        kvs.at[0:3, 0:3, 0],
         kvs.at[0:3, 0:2, 0],
-        kvs.at[0, 0:2, 0],
+        kvs.at[0, 0, 0],
         kvs.at[:, :, 0],
     ]
     for i, ref in enumerate(sent):
@@ -481,9 +469,9 @@
             dma((4, 2, 2)),
             dma((3,)),
             dma((3,)),
-            dma((4, 3)),
-            dma((4, 3)),
-            dma((2,)),
+            dma((3, 3)),
+            dma((3, 3)),
+            dma((4,)),
             dma((8,)),
             dma((3,)),
         ],

time: 70.6 us -> 69.2 us (0.980)
  Pallas kernels: 68.6 us -> 67.2 us
    pallas_call x1, Pallas kernels: 68.6 us -> 67.2 us  [body(): pl.pallas_call(kernel, out_shape=jax.ShapeDtypeStruct((rows, 128), jnp.bf...]
where the time goes in v5:
time: 69.2 us; the launch traced here: 69.1 us
  Pallas kernels  67.2 us (97%)
  local copies, waits for them, and re-layouts  1.83 us (3%)
    pallas_call x1, Pallas kernels, body(): pl.pallas_call(kernel, out_shape=jax.ShapeDtypeStruct((rows, 128), jnp.bf...  67.2 us
    unnamed x1, local copies, waits for them, and re-layouts  1.83 us

profile of v5, /device:TPU:1, one launch (start us, length us, event | category | flops | bytes accessed | tf_op | source)
XLA Modules:
  0.0 69.1 jit_solution(15653151644608446117)
XLA Ops:
  0.0 67.2 %compose.1 = bf16[1024,128]{1,0:T(8,128)(2,1)} custom-call(s32[32]{0:T(128)} %order_ref.1, bf16[1024,128]{1,0:T(8,128)(2,1)} %bitcast.8, bf16[160,512]{1,0:T(8,128)(2,1)} %bitcast.9, bf16[2560,128]{1,0:T(8,128)(2,1)} %bitcast.7), custom_call_target="tpu_custom_call" | custom-call | flops 8999999488 | bytes 2000000 | tf_op jit(solution)/shard_map/compose/pallas_call | solution.py:440
  67.2 1.8 %copy.7 = bf16[512,1,2,128]{3,2,1,0:T(2,128)(2,1)} copy(bf16[512,1,2,128]{3,2,1,0:T(2,128)(2,1)} %bitcast.6) | data formatting | bytes 524288

commit v6 on v5

--- a/solution.py
+++ b/solution.py
@@ -81,7 +81,7 @@
     across = dev(y=wrap(y + 4, NY))
 
     barrier = pltpu.get_barrier_semaphore()
-    partners = x_to + [z_next, z_prev] + g_to + [y_next, y_prev, sib, across]
+    partners = [z_next, z_prev] + g_to + [across, y_next, y_prev] + x_to + [sib]
     for to in partners:
         pl.semaphore_signal(barrier, inc=1, device_id=to, device_id_type=MESH)
 
@@ -93,7 +93,7 @@
     for cp in loads:
         cp.start()
     loads[0].wait()
-    w_wide[...] = w_ref[...].astype(jnp.float32)
+    w_wide[0:2560, :] = w_ref[...].astype(jnp.float32)
     for j in range(8):
         for half in (0, 1):
             w_heads[j, :, half * QT : (half + 1) * QT] = w_wide[pl.ds(2 * j + half, 160, stride=16), :].astype(
@@ -446,7 +446,7 @@
             pltpu.VMEM((rows, 128), jnp.bfloat16),
             pltpu.VMEM((160, 512), jnp.bfloat16),
             pltpu.VMEM((2560, 128), jnp.bfloat16),
-            pltpu.VMEM((2560, 128), jnp.float32),
+            pltpu.VMEM((2576, 128), jnp.float32),
             pltpu.VMEM((8, 160, 2 * QT), jnp.bfloat16),
             pltpu.VMEM((NG, NX, 160, QT), jnp.bfloat16),
             pltpu.VMEM((2, NX, 160, 2 * QT), jnp.bfloat16),

time: 69.2 us -> 69.5 us (level)
  no operation moved by 1% of the time
where the time goes in v6:
time: 69.5 us; the launch traced here: 69.4 us
  Pallas kernels  67.5 us (97%)
  local copies, waits for them, and re-layouts  1.83 us (3%)
    pallas_call x1, Pallas kernels, body(): pl.pallas_call(kernel, out_shape=jax.ShapeDtypeStruct((rows, 128), jnp.bf...  67.5 us
    unnamed x1, local copies, waits for them, and re-layouts  1.83 us

profile of v6, /device:TPU:1, one launch (start us, length us, event | category | flops | bytes accessed | tf_op | source)
XLA Modules:
  0.0 69.4 jit_solution(18208165624887024972)
XLA Ops:
  0.0 67.5 %compose.1 = bf16[1024,128]{1,0:T(8,128)(2,1)} custom-call(s32[32]{0:T(128)} %order_ref.1, bf16[1024,128]{1,0:T(8,128)(2,1)} %bitcast.8, bf16[160,512]{1,0:T(8,128)(2,1)} %bitcast.9, bf16[2560,128]{1,0:T(8,128)(2,1)} %bitcast.7), custom_call_target="tpu_custom_call" | custom-call | flops 8999999488 | bytes 2000000 | tf_op jit(solution)/shard_map/compose/pallas_call | solution.py:440
  67.5 1.8 %copy.7 = bf16[512,1,2,128]{3,2,1,0:T(2,128)(2,1)} copy(bf16[512,1,2,128]{3,2,1,0:T(2,128)(2,1)} %bitcast.6) | data formatting | bytes 524288
